TPU v7x, 32 devices: a whole 2x2x4 slice. The times are simulated.
32 devices in a mesh: section: 2 (over core), dp: 4 (over z), rep: 4 (over y, x).
Axes of the slice: x: 2, y: 2, z: 4, core: 2. Of those that a mesh axis runs over, the one named last changes fastest.
Arguments:
- inputs: bfloat16 [2, 8192, 768], P(None, ('dp', 'rep')), may hold values from -1.6953125 to 1.6953125
- segments: int32 [2, 8192], P(None, ('dp', 'rep')), may hold values from 0 to 8, as said below
- cotangent: bfloat16 [2, 8192, 768], P(None, ('dp', 'rep')), may hold values from -6 to 6
- w_qkv: bfloat16 [2, 768, 2304], P('section'), may hold values from -1 to 1
- b_qkv: bfloat16 [2, 2304], P('section'), may hold values from -0.796875 to 0.796875
- w_out: bfloat16 [2, 768, 768], P('section'), may hold values from -0.875 to 0.875
- b_out: bfloat16 [2, 768], P('section'), may hold values from -0.5 to 0.5
- g_attn: bfloat16 [2, 768], P('section'), may hold values from 0.5 to 1.5
- b_attn: bfloat16 [2, 768], P('section'), may hold values from -0.5 to 0.5
- w_in: bfloat16 [2, 768, 3072], P('section'), may hold values from -0.21875 to 0.21875
- b_in: bfloat16 [2, 3072], P('section'), may hold values from -0.796875 to 0.796875
- w_down: bfloat16 [2, 3072, 768], P('section'), may hold values from -0.15625 to 0.15625
- b_down: bfloat16 [2, 768], P('section'), may hold values from -0.5 to 0.5
- g_ffn: bfloat16 [2, 768], P('section'), may hold values from 0.5 to 1.5
- b_ffn: bfloat16 [2, 768], P('section'), may hold values from -0.5 to 0.5
Outputs:
- acts: bfloat16 [2, 2, 8192, 768], P('section', None, ('dp', 'rep'))
- in_grads: bfloat16 [2, 2, 8192, 768], P('section', None, ('dp', 'rep'))
- grad_w_qkv: float32 [2, 768, 2304], P('section')
- grad_b_qkv: float32 [2, 2304], P('section')
- grad_w_out: float32 [2, 768, 768], P('section')
- grad_b_out: float32 [2, 768], P('section')
- grad_g_attn: float32 [2, 768], P('section')
- grad_b_attn: float32 [2, 768], P('section')
- grad_w_in: float32 [2, 768, 3072], P('section')
- grad_b_in: float32 [2, 3072], P('section')
- grad_w_down: float32 [2, 3072, 768], P('section')
- grad_b_down: float32 [2, 768], P('section')
- grad_g_ffn: float32 [2, 768], P('section')
- grad_b_ffn: float32 [2, 768], P('section')
Inputs may be any that keep to these rules, and one draw needn't show every extreme that they name: `segments`: in every aligned run of 512 tokens of one micro-batch the live tokens come first and form whole sequences numbered 0, 1, 2, ... in order, each a multiple of 64 tokens long; the rest of the run is padding, marked 512 // 64. Some run is one sequence of all 512 tokens, and some run holds padding.
All inputs are finite; a program needn't handle non-finite values.
Results may differ from a plain program's by a relative error of at most 0.015.
Values may be sent and summed in bfloat16 or wider, within the bound.
A program may use at most 320 MiB of HBM per device.

v0:
```python
from functools import partial
import math

import jax
import jax.numpy as jnp
from jax import lax
from jax.sharding import PartitionSpec as P

D = 768
HEADS = 12
HEAD = 64
SLOT = 512
MINLEN = 64


EPSILON = 1e-05
NEG_LARGE = -1e30


def shifted(value, axis, steps):
    count = lax.axis_size(axis)
    initial, last = (max(0, -steps), min(count, count - steps))
    return lax.ppermute(value, axis, [(source, source + steps) for source in range(initial, last)])


def run_tables(seg_ids):
    length = seg_ids.shape[0]
    pad_id = SLOT // MINLEN
    same_run = seg_ids[:, None] == seg_ids[None, :]
    rows_at = lax.broadcasted_iota(jnp.int32, (length, length), 0)
    cols_at = lax.broadcasted_iota(jnp.int32, (length, length), 1)
    position = jnp.sum(
        jnp.where(same_run & (cols_at < rows_at), 1.0, 0.0).astype(jnp.float32), axis=1
    )
    allowed = same_run & (seg_ids[None, :] < pad_id) | (rows_at == cols_at)
    halfway = HEAD // 2
    column = jnp.arange(halfway).astype(jnp.float32)
    frequency = jnp.exp(column * (-2.0 * math.log(10000.0) / HEAD))
    angles = position[:, None] * frequency[None, :]
    return (jnp.cos(angles)[:, None, :], jnp.sin(angles)[:, None, :], allowed)


def rotate(vector, cos_part, sin_part):
    halfway = vector.shape[-1] // 2
    first_half = vector[..., :halfway]
    second_half = vector[..., halfway:]
    return jnp.concatenate(
        [
            first_half * cos_part - second_half * sin_part,
            second_half * cos_part + first_half * sin_part,
        ],
        axis=-1,
    )


def layer_norm(values, gain_row, shift_row):
    centered = values - jnp.mean(values, axis=-1, keepdims=True)
    spread = jnp.mean(centered * centered, axis=-1, keepdims=True)
    return centered * lax.rsqrt(spread + EPSILON) * gain_row + shift_row


def take_micro(stacked, micro_index):
    bounded = jnp.clip(micro_index, 0, stacked.shape[0] - 1)
    return lax.dynamic_index_in_dim(stacked, bounded, 0, keepdims=False)


def choose_micro(candidates, micro_index):
    chosen = candidates[0]
    chosen = jax.tree.map(partial(jnp.where, micro_index == 1), candidates[1], chosen)
    return chosen


def forward_layer(source, tables, weights):
    cos_part, sin_part, allowed = tables
    w_qkv, b_qkv, w_out, b_out, g_attn, b_attn, w_in, b_in, w_down, b_down, g_ffn, b_ffn = weights
    length = source.shape[0]
    score_scale = 1.0 / math.sqrt(HEAD)
    joined = jnp.dot(source, w_qkv, preferred_element_type=jnp.float32) + b_qkv.astype(jnp.float32)
    split_heads = joined.reshape(length, 3, HEADS, HEAD)
    queries = rotate(split_heads[:, 0], cos_part, sin_part).astype(jnp.bfloat16)
    keys_rot = rotate(split_heads[:, 1], cos_part, sin_part).astype(jnp.bfloat16)
    values = split_heads[:, 2].astype(jnp.bfloat16)
    scores = (
        jnp.einsum("qhd,khd->hqk", queries, keys_rot, preferred_element_type=jnp.float32)
        * score_scale
    )
    scores = jnp.where(allowed[None], scores, NEG_LARGE)
    peak_score = jnp.max(scores, axis=-1, keepdims=True)
    exponent = jnp.exp(scores - peak_score)
    row_total = jnp.sum(exponent, axis=-1, keepdims=True)
    probabilities = exponent / row_total
    log_total = peak_score + jnp.log(row_total)
    attended = jnp.einsum(
        "hqk,khd->qhd",
        probabilities.astype(jnp.bfloat16),
        values,
        preferred_element_type=jnp.float32,
    )
    attended = attended.reshape(length, D).astype(jnp.bfloat16)
    branch = jnp.dot(attended, w_out, preferred_element_type=jnp.float32) + b_out.astype(
        jnp.float32
    )
    residual_one = source.astype(jnp.float32) + branch
    normed = layer_norm(residual_one, g_attn.astype(jnp.float32), b_attn.astype(jnp.float32))
    normed_low = normed.astype(jnp.bfloat16)
    expanded = jnp.dot(normed_low, w_in, preferred_element_type=jnp.float32) + b_in.astype(
        jnp.float32
    )
    activated = jax.nn.gelu(expanded, approximate=True).astype(jnp.bfloat16)
    branch_two = jnp.dot(activated, w_down, preferred_element_type=jnp.float32) + b_down.astype(
        jnp.float32
    )
    residual_two = normed + branch_two
    produced = layer_norm(
        residual_two, g_ffn.astype(jnp.float32), b_ffn.astype(jnp.float32)
    ).astype(jnp.bfloat16)
    stashed = (
        source,
        queries,
        keys_rot,
        values,
        log_total,
        attended,
        residual_one,
        normed_low,
        expanded,
        activated,
        residual_two,
    )
    return (produced, stashed)


def backward_ffn(stashed, upstream, weights):
    (
        source,
        queries,
        keys_rot,
        values,
        log_total,
        attended,
        residual_one,
        normed_low,
        expanded,
        activated,
        residual_two,
    ) = stashed
    w_qkv, b_qkv, w_out, b_out, g_attn, b_attn, w_in, b_in, w_down, b_down, g_ffn, b_ffn = weights
    norm_pull = jax.vjp(
        layer_norm, residual_two, g_ffn.astype(jnp.float32), b_ffn.astype(jnp.float32)
    )[1]
    grad_res_two, grad_g_ffn, grad_b_ffn = norm_pull(upstream)
    grad_branch_two = grad_res_two.astype(jnp.bfloat16)
    grad_b_down = jnp.sum(grad_branch_two.astype(jnp.float32), axis=0)
    grad_w_down = jnp.einsum(
        "tf,td->fd", activated, grad_branch_two, preferred_element_type=jnp.float32
    )
    grad_activated = jnp.einsum(
        "td,fd->tf", grad_branch_two, w_down, preferred_element_type=jnp.float32
    )
    gelu_pull = jax.vjp(partial(jax.nn.gelu, approximate=True), expanded)[1]
    grad_expanded = gelu_pull(grad_activated)[0].astype(jnp.bfloat16)
    grad_b_in = jnp.sum(grad_expanded.astype(jnp.float32), axis=0)
    grad_w_in = jnp.einsum(
        "td,tf->df", normed_low, grad_expanded, preferred_element_type=jnp.float32
    )
    grad_normed = grad_res_two + jnp.einsum(
        "tf,df->td", grad_expanded, w_in, preferred_element_type=jnp.float32
    )
    return (grad_normed, (grad_w_in, grad_b_in, grad_w_down, grad_b_down, grad_g_ffn, grad_b_ffn))


def backward_attn(stashed, grad_normed, tables, weights):
    cos_part, sin_part, allowed = tables
    (
        source,
        queries,
        keys_rot,
        values,
        log_total,
        attended,
        residual_one,
        normed_low,
        expanded,
        activated,
        residual_two,
    ) = stashed
    w_qkv, b_qkv, w_out, b_out, g_attn, b_attn, w_in, b_in, w_down, b_down, g_ffn, b_ffn = weights
    length = source.shape[0]
    score_scale = 1.0 / math.sqrt(HEAD)
    norm_pull_one = jax.vjp(
        layer_norm, residual_one, g_attn.astype(jnp.float32), b_attn.astype(jnp.float32)
    )[1]
    grad_res_one, grad_g_attn, grad_b_attn = norm_pull_one(grad_normed)
    grad_branch = grad_res_one.astype(jnp.bfloat16)
    grad_b_out = jnp.sum(grad_branch.astype(jnp.float32), axis=0)
    grad_w_out = jnp.einsum("te,td->ed", attended, grad_branch, preferred_element_type=jnp.float32)
    grad_attended = jnp.einsum("td,ed->te", grad_branch, w_out, preferred_element_type=jnp.float32)
    grad_attended = grad_attended.astype(jnp.bfloat16).reshape(length, HEADS, HEAD)
    scores = (
        jnp.einsum("qhd,khd->hqk", queries, keys_rot, preferred_element_type=jnp.float32)
        * score_scale
    )
    scores = jnp.where(allowed[None], scores, NEG_LARGE)
    probabilities = jnp.exp(scores - log_total)
    grad_probs = jnp.einsum(
        "qhd,khd->hqk", grad_attended, values, preferred_element_type=jnp.float32
    )
    grad_values = jnp.einsum(
        "hqk,qhd->khd",
        probabilities.astype(jnp.bfloat16),
        grad_attended,
        preferred_element_type=jnp.float32,
    )
    inner_sum = jnp.sum(probabilities * grad_probs, axis=-1, keepdims=True)
    grad_scores = jnp.where(allowed[None], probabilities * (grad_probs - inner_sum), 0.0).astype(
        jnp.bfloat16
    )
    grad_queries = (
        jnp.einsum("hqk,khd->qhd", grad_scores, keys_rot, preferred_element_type=jnp.float32)
        * score_scale
    )
    grad_keys = (
        jnp.einsum("hqk,qhd->khd", grad_scores, queries, preferred_element_type=jnp.float32)
        * score_scale
    )
    grad_joined = jnp.stack(
        [
            rotate(grad_queries, cos_part, -sin_part),
            rotate(grad_keys, cos_part, -sin_part),
            grad_values,
        ],
        axis=1,
    )
    grad_joined = grad_joined.reshape(length, 3 * D).astype(jnp.bfloat16)
    grad_b_qkv = jnp.sum(grad_joined.astype(jnp.float32), axis=0)
    grad_w_qkv = jnp.einsum("td,te->de", source, grad_joined, preferred_element_type=jnp.float32)
    grad_source = grad_res_one + jnp.einsum(
        "te,de->td", grad_joined, w_qkv, preferred_element_type=jnp.float32
    )
    return (
        grad_source.astype(jnp.bfloat16),
        (grad_w_qkv, grad_b_qkv, grad_w_out, grad_b_out, grad_g_attn, grad_b_attn),
    )


def per_device(
    inputs,
    segments,
    cotangent,
    w_qkv,
    b_qkv,
    w_out,
    b_out,
    g_attn,
    b_attn,
    w_in,
    b_in,
    w_down,
    b_down,
    g_ffn,
    b_ffn,
):
    section_id = lax.axis_index("section")
    section_count = lax.axis_size("section")
    weights = tuple(
        (
            weight_arg[0]
            for weight_arg in (
                w_qkv,
                b_qkv,
                w_out,
                b_out,
                g_attn,
                b_attn,
                w_in,
                b_in,
                w_down,
                b_down,
                g_ffn,
                b_ffn,
            )
        )
    )
    micro_count = inputs.shape[0]
    turn_count = micro_count + section_count - 1
    pad_id = SLOT // MINLEN
    blank = jnp.zeros(inputs.shape[1:], jnp.bfloat16)
    layer_inputs = [blank] * micro_count
    layer_outputs = [blank] * micro_count
    incoming = blank
    for turn_index in range(turn_count):
        micro_index = turn_index - section_id
        own_input = inputs[min(turn_index, micro_count - 1)]
        source = jnp.where(section_id == 0, own_input, incoming)
        tables = run_tables(take_micro(segments, micro_index))
        produced, stashed = forward_layer(source, tables, weights)
        for position in range(micro_count):
            is_match = micro_index == position
            layer_inputs[position] = jnp.where(is_match, source, layer_inputs[position])
            layer_outputs[position] = jnp.where(is_match, produced, layer_outputs[position])
        if turn_index + 1 < turn_count:
            incoming = shifted(produced, "section", 1)
    incoming = blank
    in_grads = [blank] * micro_count
    running_ffn = None
    running_attn = None
    for turn_index in range(turn_count):
        micro_index = turn_index - (section_count - 1 - section_id)
        is_valid = (micro_index >= 0) & (micro_index < micro_count)
        run_segments = take_micro(segments, micro_index)
        tables = run_tables(run_segments)
        real_rows = jnp.where(run_segments < pad_id, 1.0, 0.0).astype(jnp.float32)[:, None]
        last_grad = take_micro(cotangent, micro_index).astype(jnp.float32) * real_rows
        upstream = jnp.where(
            section_id == section_count - 1, last_grad, incoming.astype(jnp.float32)
        )
        stashed = forward_layer(choose_micro(layer_inputs, micro_index), tables, weights)[1]
        grad_normed, ffn_grads = backward_ffn(stashed, upstream, weights)
        ffn_grads = tuple((jnp.where(is_valid, part_grad, 0.0) for part_grad in ffn_grads))
        if turn_index == 0:
            running_ffn = ffn_grads
        else:
            running_ffn = tuple(
                (older_sum + newer_sum for older_sum, newer_sum in zip(running_ffn, ffn_grads))
            )
        grad_source, attn_grads = backward_attn(stashed, grad_normed, tables, weights)
        attn_grads = tuple((jnp.where(is_valid, part_grad, 0.0) for part_grad in attn_grads))
        if turn_index == 0:
            running_attn = attn_grads
        else:
            running_attn = tuple(
                (older_sum + newer_sum for older_sum, newer_sum in zip(running_attn, attn_grads))
            )
        for position in range(micro_count):
            in_grads[position] = jnp.where(micro_index == position, grad_source, in_grads[position])
        if turn_index + 1 < turn_count:
            incoming = shifted(grad_source, "section", -1)
    running = (
        lax.psum_scatter(running_attn[0], ("dp", "rep"), scatter_dimension=0, tiled=True),
        lax.psum_scatter(running_attn[1], ("dp", "rep"), scatter_dimension=0, tiled=True),
        lax.psum_scatter(running_attn[2], ("dp", "rep"), scatter_dimension=0, tiled=True),
        lax.psum_scatter(running_attn[3], ("dp", "rep"), scatter_dimension=0, tiled=True),
        lax.psum_scatter(running_attn[4], ("dp", "rep"), scatter_dimension=0, tiled=True),
        lax.psum_scatter(running_attn[5], ("dp", "rep"), scatter_dimension=0, tiled=True),
        lax.psum_scatter(running_ffn[0], ("dp", "rep"), scatter_dimension=0, tiled=True),
        lax.psum_scatter(running_ffn[1], ("dp", "rep"), scatter_dimension=0, tiled=True),
        lax.psum_scatter(running_ffn[2], ("dp", "rep"), scatter_dimension=0, tiled=True),
        lax.psum_scatter(running_ffn[3], ("dp", "rep"), scatter_dimension=0, tiled=True),
        lax.psum_scatter(running_ffn[4], ("dp", "rep"), scatter_dimension=0, tiled=True),
        lax.psum_scatter(running_ffn[5], ("dp", "rep"), scatter_dimension=0, tiled=True),
    )
    gathered = (
        lax.all_gather(running[0].astype(jnp.bfloat16), ("dp", "rep"), axis=0, tiled=True).astype(
            jnp.float32
        ),
        lax.all_gather(running[1].astype(jnp.bfloat16), ("dp", "rep"), axis=0, tiled=True).astype(
            jnp.float32
        ),
        lax.all_gather(running[2].astype(jnp.bfloat16), ("dp", "rep"), axis=0, tiled=True).astype(
            jnp.float32
        ),
        lax.all_gather(running[3].astype(jnp.bfloat16), ("dp", "rep"), axis=0, tiled=True).astype(
            jnp.float32
        ),
        lax.all_gather(running[4].astype(jnp.bfloat16), ("dp", "rep"), axis=0, tiled=True).astype(
            jnp.float32
        ),
        lax.all_gather(running[5].astype(jnp.bfloat16), ("dp", "rep"), axis=0, tiled=True).astype(
            jnp.float32
        ),
        lax.all_gather(running[6].astype(jnp.bfloat16), ("dp", "rep"), axis=0, tiled=True).astype(
            jnp.float32
        ),
        lax.all_gather(running[7].astype(jnp.bfloat16), ("dp", "rep"), axis=0, tiled=True).astype(
            jnp.float32
        ),
        lax.all_gather(running[8].astype(jnp.bfloat16), ("dp", "rep"), axis=0, tiled=True).astype(
            jnp.float32
        ),
        lax.all_gather(running[9].astype(jnp.bfloat16), ("dp", "rep"), axis=0, tiled=True).astype(
            jnp.float32
        ),
        lax.all_gather(running[10].astype(jnp.bfloat16), ("dp", "rep"), axis=0, tiled=True).astype(
            jnp.float32
        ),
        lax.all_gather(running[11].astype(jnp.bfloat16), ("dp", "rep"), axis=0, tiled=True).astype(
            jnp.float32
        ),
    )
    acts = jnp.stack(layer_outputs)[None]
    grads_input = jnp.stack(in_grads)[None]
    return (
        acts,
        grads_input,
        gathered[0][None],
        gathered[1][None],
        gathered[2][None],
        gathered[3][None],
        gathered[4][None],
        gathered[5][None],
        gathered[6][None],
        gathered[7][None],
        gathered[8][None],
        gathered[9][None],
        gathered[10][None],
        gathered[11][None],
    )


def solution(mesh):
    placed = (
        P(None, ("dp", "rep"), None),
        P(None, ("dp", "rep")),
        P(None, ("dp", "rep"), None),
        P("section", None, None),
        P("section", None),
        P("section", None, None),
        P("section", None),
        P("section", None),
        P("section", None),
        P("section", None, None),
        P("section", None),
        P("section", None, None),
        P("section", None),
        P("section", None),
        P("section", None),
    )
    return jax.shard_map(
        per_device,
        mesh=mesh,
        in_specs=placed,
        out_specs=(
            P("section", None, ("dp", "rep"), None),
            P("section", None, ("dp", "rep"), None),
            P("section", None, None),
            P("section", None),
            P("section", None, None),
            P("section", None),
            P("section", None),
            P("section", None),
            P("section", None, None),
            P("section", None),
            P("section", None, None),
            P("section", None),
            P("section", None),
            P("section", None),
        ),
        check_vma=False,
    )
```

profile of v0, /device:TPU:0, one launch (start us, length us, event | category | flops | bytes accessed | tf_op | source)
XLA Modules:
  0.0 1402.4 jit_solution(1669361920840409181)
XLA Ops:
  32.9 11.2 fusion.458
  51.9 7.4 fusion.73
  82.4 11.3 fusion.461
  185.6 8.1 fusion.357
  200.9 20.6 %multiply_bitcast_fusion.5 = f32[512,12,64]{0,2,1:T(8,128)} fusion(f32[12,512,512]{1,2,0:T(8,128)} %fusion.357, f32[12,512,512]{1,2,0:T(8,128)} %copy-done.17, f32[12,512]{1,0:T(8,128)} %log_add_fusion.2, pred[512,512]{0,1:T(8,128)(4,1)} %get-tuple-element.252, bf16[512,12,32]{0,2,1:T(8,128)(2,1)} %copy-done.92, bf16[512,12,32]{0,2,1:T(8,128)(2,1)} %copy-done.93), kind=kOutput, calls=%fused_computation.310 | convolution fusion | flops 439228928 | bytes 27811840 | tf_op jit(solution)/shard_map/hqk,khd->qhd/dot_general | solution.py:219
  221.5 21.3 %multiply_bitcast_fusion.4 = f32[512,12,64]{0,2,1:T(8,128)} fusion(f32[12,512,512]{1,2,0:T(8,128)} %fusion.357, f32[12,512,512]{1,2,0:T(8,128)} %copy-done.17, f32[12,512]{1,0:T(8,128)} %log_add_fusion.2, pred[512,512]{0,1:T(8,128)(4,1)} %get-tuple-element.252, bf16[512,12,32]{0,2,1:T(8,128)(2,1)} %copy-done.91, bf16[512,12,32]{0,2,1:T(8,128)(2,1)} %copy-done.90), kind=kOutput, calls=%fused_computation.309 | convolution fusion | flops 439228928 | bytes 27811840 | tf_op jit(solution)/shard_map/hqk,qhd->khd/dot_general | solution.py:223
  356.0 8.2 fusion.354
  371.4 20.6 %multiply_bitcast_fusion.3 = f32[512,12,64]{0,2,1:T(8,128)} fusion(f32[12,512,512]{1,2,0:T(8,128)} %fusion.354, f32[12,512,512]{1,2,0:T(8,128)} %copy-done.16, f32[12,512]{1,0:T(8,128)} %log_add_fusion.1, pred[512,512]{0,1:T(8,128)(4,1)} %get-tuple-element.251, bf16[512,12,32]{0,2,1:T(8,128)(2,1)} %copy-done.88, bf16[512,12,32]{0,2,1:T(8,128)(2,1)} %copy-done.89), kind=kOutput, calls=%fused_computation.300 | convolution fusion | flops 439228928 | bytes 27811840 | tf_op jit(solution)/shard_map/hqk,khd->qhd/dot_general | solution.py:219
  392.0 21.5 %multiply_bitcast_fusion.2 = f32[512,12,64]{0,2,1:T(8,128)} fusion(f32[12,512,512]{1,2,0:T(8,128)} %fusion.354, f32[12,512,512]{1,2,0:T(8,128)} %copy-done.16, f32[12,512]{1,0:T(8,128)} %log_add_fusion.1, pred[512,512]{0,1:T(8,128)(4,1)} %get-tuple-element.251, bf16[512,12,32]{0,2,1:T(8,128)(2,1)} %copy-done.87, bf16[512,12,32]{0,2,1:T(8,128)(2,1)} %copy-done.86), kind=kOutput, calls=%fused_computation.299 | convolution fusion | flops 439228928 | bytes 27811840 | tf_op jit(solution)/shard_map/hqk,qhd->khd/dot_general | solution.py:223
  461.0 8.1 fusion.351
  469.0 21.2 %multiply_bitcast_fusion.1 = f32[512,12,64]{0,2,1:T(8,128)} fusion(f32[12,512,512]{1,2,0:T(8,128)} %fusion.351, f32[12,512,512]{1,2,0:T(8,128)} %copy-done.15, f32[12,512]{1,0:T(8,128)} %log_add_fusion, pred[512,512]{0,1:T(8,128)(4,1)} %get-tuple-element.250, bf16[512,12,32]{0,2,1:T(8,128)(2,1)} %copy-done.84, bf16[512,12,32]{0,2,1:T(8,128)(2,1)} %copy-done.85), kind=kOutput, calls=%fused_computation.290 | convolution fusion | flops 439228928 | bytes 27811840 | tf_op jit(solution)/shard_map/hqk,khd->qhd/dot_general | solution.py:219
  490.2 21.3 %multiply_bitcast_fusion = f32[512,12,64]{0,2,1:T(8,128)} fusion(f32[12,512,512]{1,2,0:T(8,128)} %fusion.351, f32[12,512,512]{1,2,0:T(8,128)} %copy-done.15, f32[12,512]{1,0:T(8,128)} %log_add_fusion, pred[512,512]{0,1:T(8,128)(4,1)} %get-tuple-element.250, bf16[512,12,32]{0,2,1:T(8,128)(2,1)} %copy-done.83, bf16[512,12,32]{0,2,1:T(8,128)(2,1)} %copy-done.82), kind=kOutput, calls=%fused_computation.289 | convolution fusion | flops 439228928 | bytes 27811840 | tf_op jit(solution)/shard_map/hqk,qhd->khd/dot_general | solution.py:223
  540.7 9.0 select_add_fusion.1
  550.0 10.4 fusion.447
  560.5 10.3 fusion.448
  570.8 9.2 select_add_fusion
  582.5 154.7 %reduce-scatter.5.cloned.1.call-done = f32[48,2304]{1,0:T(8,128)} async-done(((f32[768,2304]{1,0:T(8,128)}), f32[48,2304]{1,0:T(8,128)}) %reduce-scatter.5.cloned.1.call-update) | async-done | bytes 442384 | tf_op jit(solution)/shard_map/reduce_scatter | solution.py:339
  739.0 175.7 %reduce-scatter.9.cloned.1.call-done = f32[48,3072]{1,0:T(8,128)} async-done(((f32[768,3072]{1,0:T(8,128)}), f32[48,3072]{1,0:T(8,128)}) %reduce-scatter.9.cloned.1.call-update) | async-done | bytes 589840 | tf_op jit(solution)/shard_map/reduce_scatter | solution.py:345
  937.1 11.3 fusion.464
  955.6 135.4 %reduce-scatter.11.cloned.1.call-done = f32[192,768]{1,0:T(8,128)} async-done(((f32[3072,768]{1,0:T(8,128)}), f32[192,768]{1,0:T(8,128)}) %reduce-scatter.11.cloned.1.call-update) | async-done | bytes 589840 | tf_op jit(solution)/shard_map/reduce_scatter | solution.py:347
  1120.9 76.3 %all-reduce.16 = (bf16[2304]{0:T(1024)(128)(2,1)}, bf16[768]{0:T(1024)(128)(2,1)}, bf16[768]{0:T(1024)(128)(2,1)}, bf16[768]{0:T(1024)(128)(2,1)}, bf16[3072]{0:...) all-reduce(f32[2304]{0:T(1024)S(1)} %add.757, ...), channel_id=3, replica_groups=mesh['section'=2,'dp'=4,'rep'=4] {'dp','rep'}, use_global_device_ids=true, to_apply=%region_61.62.clone | all-reduce | flops 9984 | bytes 59904
  1212.3 72.9 %all-reduce.17 = (bf16[2304]{0:T(1024)(128)(2,1)}, bf16[768]{0:T(1024)(128)(2,1)}, bf16[768]{0:T(1024)(128)(2,1)}, bf16[768]{0:T(1024)(128)(2,1)}, bf16[3072]{0:...) all-reduce(bf16[2304]{0:T(1024)(128)(2,1)S(1)} %dynamic-update-slic, ...), channel_id=1, replica_groups=mesh['section'=2,'dp'=4,'rep'=4] {'dp','rep'}, use_global_device_ids=true, to_apply=%add | all-reduce | flops 9984 | bytes 39936
  1309.7 7.4 bitcast_convert_fusion.1
  1317.1 71.2 %all-gather.11.cloned.1.call-done = bf16[3072,768]{1,0:T(8,128)(2,1)} async-done(((bf16[192,768]{1,0:T(8,128)(2,1)}), bf16[3072,768]{1,0:T(8,128)(2,1)}) %all-gather.11.cloned.1.call-update) | async-done | bytes 4718608 | tf_op jit(solution)/shard_map/all_gather | solution.py:377
  (763 shorter events, 456.0 us)
Async XLA Ops:
  7.2 573.7 %reduce-scatter.7.cloned.1.call-start = ((), (), s32[]{:S(2)}) async-start(), calls=%async_computation.6 | async-start | bytes 2506752 | tf_op jit(solution)/shard_map/reduce_scatter | solution.py:341
  8.8 50.6 %copy-start.183 = (f32[768]{0:T(1024)}, f32[768]{0:T(1024)S(1)}, u32[]{:S(2)}) copy-start(f32[768]{0:T(1024)S(1)} %convert_reduce_fusion.15) | copy-start | bytes 9220
  10.8 39.7 %copy-start.189 = (f32[768]{0:T(1024)}, f32[768]{0:T(1024)S(1)}, u32[]{:S(2)}) copy-start(f32[768]{0:T(1024)S(1)} %convert_reduce_fusion.18) | copy-start | bytes 9220
  62.6 102.8 %copy-start.79 = (f32[768]{0:T(1024)}, f32[768]{0:T(1024)S(1)}, u32[]{:S(2)}) copy-start(f32[768]{0:T(1024)S(1)} %get-tuple-element.265) | copy-start | bytes 9220
  62.9 4.3 collective-permute-start
  113.5 8.8 collective-permute-start.1
  153.6 24.4 %copy-start.23 = (f32[512,768]{1,0:T(8,128)}, f32[512,768]{1,0:T(8,128)S(1)}, u32[]{:S(2)}) copy-start(f32[512,768]{1,0:T(8,128)S(1)} %get-tuple-element.234) | copy-start | bytes 4718596
  153.6 24.4 %copy-start.131 = (f32[512]{0:T(512)}, f32[512]{0:T(512)S(1)}, u32[]{:S(2)}) copy-start(f32[512]{0:T(512)S(1)} %broadcast_multiply_fusion.5) | copy-start | bytes 6148
  154.0 24.0 %copy-start.171 = (f32[512]{0:T(512)}, f32[512]{0:T(512)S(1)}, u32[]{:S(2)}) copy-start(f32[512]{0:T(512)S(1)} %fusion.363) | copy-start | bytes 6148
  288.1 43.5 %collective-permute-start.2 = (bf16[512,768]{1,0:T(8,128)(2,1)}, bf16[512,768]{1,0:T(8,128)(2,1)}, u32[]{:S(2)}, u32[]{:S(2)}) collective-permute-start(bf16[512,768]{1,0:T(8,128)(2,1)} %add_convert_fusion.2), channel_id=1, source_target_pairs={{16,0},{17,1},{18,2},{19,3},{20,4},{21,5},{22,6},{23,7},{24,8},{25... | collective-permute-start | bytes 2359304 | tf_op jit(solution)/shard_map/ppermute | solution.py:23
  318.3 19.2 %slice-start.24 = ((s8[6291456]{0:T(1024)(128)(4,1)}), s8[4194304]{0:T(1024)(128)(4,1)S(1)}, s32[]{:S(2)}) async-start(s8[6291456]{0:T(1024)(128)(4,1)} %bitcast.474), calls=%async_computation.36 | async-start | bytes 8388608
  323.6 13.9 slice-start.25
  413.6 17.9 %slice-start.26 = ((s8[6291456]{0:T(1024)(128)(4,1)}), s8[4194304]{0:T(1024)(128)(4,1)S(1)}, s32[]{:S(2)}) async-start(s8[6291456]{0:T(1024)(128)(4,1)} %bitcast.476), calls=%async_computation.38 | async-start | bytes 8388608
  419.8 7.3 collective-permute-start.3
  448.5 288.8 %reduce-scatter.5.cloned.1.call-start = ((), (), s32[]{:S(2)}) async-start(), calls=%async_computation.4 | async-start | bytes 7520256 | tf_op jit(solution)/shard_map/reduce_scatter | solution.py:339
  528.9 385.8 %reduce-scatter.9.cloned.1.call-start = ((), (), s32[]{:S(2)}) async-start(), calls=%async_computation.8 | async-start | bytes 10027008 | tf_op jit(solution)/shard_map/reduce_scatter | solution.py:345
  549.8 541.3 %reduce-scatter.11.cloned.1.call-start = ((), (), s32[]{:S(2)}) async-start(), calls=%async_computation.10 | async-start | bytes 10027008 | tf_op jit(solution)/shard_map/reduce_scatter | solution.py:347
  550.0 20.8 %slice-start.28 = ((s8[6291456]{0:T(1024)(128)(4,1)}), s8[4194304]{0:T(1024)(128)(4,1)S(1)}, s32[]{:S(2)}) async-start(s8[6291456]{0:T(1024)(128)(4,1)} %bitcast.478), calls=%async_computation.40 | async-start | bytes 8388608
  580.0 336.8 %copy-start.199 = (u32[32]{0:T(128)S(1)}, u32[32]{0:T(128)}, u32[]{:S(2)}) copy-start(u32[32]{0:T(128)} %constant.128) | copy-start | bytes 388
  580.1 721.3 %all-gather.7.cloned.1.call-start = ((), (), s32[]{:S(2)}) async-start(), calls=%async_computation.7 | async-start | bytes 1253376 | tf_op jit(solution)/shard_map/all_gather | solution.py:359
  582.5 721.8 %all-gather.5.cloned.1.call-start = ((), (), s32[]{:S(2)}) async-start(), calls=%async_computation.5 | async-start | bytes 3760128 | tf_op jit(solution)/shard_map/all_gather | solution.py:353
  739.0 570.7 %all-gather.9.cloned.1.call-start = ((), (), s32[]{:S(2)}) async-start(), calls=%async_computation.9 | async-start | bytes 5013504 | tf_op jit(solution)/shard_map/all_gather | solution.py:371
  916.6 471.8 %all-gather.11.cloned.1.call-start = ((), (), s32[]{:S(2)}) async-start(), calls=%async_computation.11 | async-start | bytes 5013504 | tf_op jit(solution)/shard_map/all_gather | solution.py:377
  948.3 144.5 %copy-start.194 = (f32[768]{0:T(1024)S(1)}, f32[768]{0:T(1024)}, u32[]{:S(2)}) copy-start(f32[768]{0:T(1024)} %copy-done.189) | copy-start | bytes 9220
  (232 other events, 1043.8 us)
Sparse Core Ops, SparseCore 0:
  448.6 132.2 reduce-scatter.6
  587.7 149.5 reduce-scatter.4
  744.4 170.2 reduce-scatter.8
  920.8 170.1 reduce-scatter.10
  1094.1 55.1 all-gather.6
  1152.3 70.9 all-gather.4
  1226.5 78.8 all-gather.8
  1309.2 79.1 all-gather.10
where the time goes:
time: 1410 us; the launch traced here: 1400 us
  waiting for transfers between devices  539 us (38%)
  matrix products  461 us (33%)
  blocking collectives  149 us (11%)
  other arithmetic  120 us (9%)
  local copies, waits for them, and re-layouts  102 us (7%)
  between operations  21.7 us (2%)
    reduce_scatter x1, waiting for transfers between devices, per_device(): lax.psum_scatter(running_ffn[0], ('dp', 'rep'), scatter_dimension=0, tile...  176 us
    reduce_scatter x1, waiting for transfers between devices, per_device(): lax.psum_scatter(running_attn[0], ('dp', 'rep'), scatter_dimension=0, til...  155 us
    unnamed x2, blocking collectives  149 us
    reduce_scatter x1, waiting for transfers between devices, per_device(): lax.psum_scatter(running_ffn[2], ('dp', 'rep'), scatter_dimension=0, tile...  135 us
    all_gather x1, waiting for transfers between devices, per_device(): lax.all_gather(running[8].astype(jnp.bfloat16), ('dp', 'rep'), axis=0, ti...  71.2 us
    dot_general x3, matrix products, backward_attn(): jnp.einsum('hqk,qhd->khd', grad_scores, queries, preferred_element_type=j...  64.2 us
    dot_general x3, matrix products, backward_attn(): jnp.einsum('hqk,khd->qhd', grad_scores, keys_rot, preferred_element_type=...  62.4 us
    dot_general x6, matrix products, forward_layer(): jnp.dot(normed_low, w_in, preferred_element_type=jnp.float32)  37 us
  transfers between devices with their start and end apart: 12, of which 6 were waited for; matrix products, arithmetic and copies ran while one was open for 21% of the time, Pallas kernels for 0%

commit v1 on v0

v1 whole, which is shorter than its diff:
```python
import functools
import math

import jax
import jax.numpy as jnp
from jax import lax
from jax.experimental import pallas as pl
from jax.experimental.pallas import tpu as pltpu
from jax.sharding import PartitionSpec as P

D = 768
HEADS = 12
HEAD = 64
PAIRS = HEADS // 2
SLOT = 512
MINLEN = 64
CHUNKS = 4
OUT = 2 * CHUNKS
QKV = OUT + 1
BLOCKS = QKV + 3
SEND_ORDER = (9, 10, 11, 8, 1, 0, 3, 2, 5, 4, 7, 6)
B_QKV, B_OUT, G_ATTN, B_ATTN, B_IN, B_DOWN, G_FFN, B_FFN = 0, 3, 4, 5, 6, 10, 11, 12
SMALL = 16
EPSILON = 1e-05
NEG_LARGE = -1e30
LOG2E = math.log2(math.e)
SCORE = LOG2E / math.sqrt(HEAD)
GELU_A = math.sqrt(2.0 / math.pi)
GELU_B = 0.044715
HALF = D // 2
MESH = pl.DeviceIdType.MESH
F32 = jnp.float32
BF16 = jnp.bfloat16
VMEM_LIMIT = 62 * 1024 * 1024


def dot(a, b):
    return lax.dot_general(a, b, (((1,), (0,)), ((), ())), preferred_element_type=F32)


def dot_t(a, b):
    return lax.dot_general(a, b, (((1,), (1,)), ((), ())), preferred_element_type=F32)


def swap_halves(t):
    lane = lax.broadcasted_iota(jnp.int32, t.shape, 1)
    return jnp.where(lane % HEAD < HEAD // 2, pltpu.roll(t, 96, 1), pltpu.roll(t, 32, 1))


def low_lanes(shape):
    return lax.broadcasted_iota(jnp.int32, shape, 1) < HEAD


def gelu_parts(u):
    square = u * u
    t = jnp.tanh(GELU_A * u * (1.0 + GELU_B * square))
    return square, t


def forward_kernel(
    inp, segr, segc, wq, wo, wi, wd, small,
    wall, xs, qkvs, lses, atts, n1s, nbs, us, n2s, rss, tabs, biases, acts, smalls,
    W, SM, X, QK, LSE, ATT, N1, NB, U, N2, RS, TAB, BIAS, ACC, ACT,
    osem, rsend, rrecv, ssem, wsem, stash, asem,
):
    sec = lax.axis_index("section")
    other = 1 - sec
    peer = {"section": other}
    tokens = X.shape[1]

    def source(b):
        if b < OUT:
            part = pl.ds(b // 2 * D, D)
            return wd.at[0, part, :] if b % 2 == 0 else wi.at[0, :, part]
        if b == OUT:
            return wo.at[0]
        return wq.at[0, :, pl.ds((b - QKV) * D, D)]

    def own_copy(b):
        return pltpu.make_async_copy(source(b), W.at[sec, b], osem.at[b])

    def peer_copy(b):
        return pltpu.make_async_remote_copy(
            source(b), W.at[sec, b], rsend.at[b], rrecv.at[b], device_id=peer, device_id_type=MESH
        )

    load_x = pltpu.make_async_copy(inp.at[sec], X.at[0], ssem.at[0])
    load_x.start()
    for b in SEND_ORDER[:4]:
        own_copy(b).start()
    barrier = pltpu.get_barrier_semaphore()
    pl.semaphore_signal(barrier, inc=1, device_id=peer, device_id_type=MESH)
    pl.semaphore_wait(barrier, 1)
    small_copy = pltpu.make_async_remote_copy(
        small, SM.at[sec], ssem.at[1], ssem.at[2], device_id=peer, device_id_type=MESH
    )
    small_copy.start()
    for b in SEND_ORDER:
        peer_copy(b).start()
    for b in SEND_ORDER[4:]:
        own_copy(b).start()
    SM[sec] = small[...]

    row_at = lax.broadcasted_iota(jnp.int32, (tokens, tokens), 0)
    col_at = lax.broadcasted_iota(jnp.int32, (tokens, tokens), 1)
    seg_col = segc[...]
    seg_row = segr[...]
    same = seg_col == seg_row
    position = jnp.sum(jnp.where(same & (col_at < row_at), 1.0, 0.0), axis=1, keepdims=True)
    allowed = (same & (seg_col < SLOT // MINLEN)) | (row_at == col_at)
    BIAS[...] = jnp.where(allowed, 0.0, NEG_LARGE)
    lane = lax.broadcasted_iota(jnp.int32, (1, 128), 1)
    frequency = jnp.exp((lane % 32).astype(F32) * (-2.0 * math.log(10000.0) / HEAD))
    angle = position * frequency
    TAB[0] = jnp.cos(angle)
    sine = jnp.sin(angle)
    TAB[1] = jnp.where(lane % HEAD < HEAD // 2, -sine, sine)
    table_out = pltpu.make_async_copy(TAB, tabs, ssem.at[3])
    table_out.start()
    bias_out = pltpu.make_async_copy(BIAS, biases, ssem.at[4])
    bias_out.start()
    load_x.wait()
    small_copy.wait()
    small_out = pltpu.make_async_copy(SM, smalls, ssem.at[5])
    small_out.start()

    def keep(k, layer, src, dst):
        pltpu.make_async_copy(src.at[layer], dst.at[layer], stash.at[layer, k]).start()

    def layer_step(layer, _):
        def ready(b):
            @pl.when(layer == sec)
            def _():
                pltpu.make_async_copy(wo.at[0], W.at[sec, b], osem.at[b]).wait()

            @pl.when(layer != sec)
            def _():
                pltpu.make_async_remote_copy(
                    wo.at[0], W.at[other, b], rsend.at[b], rrecv.at[b], device_id=peer, device_id_type=MESH
                ).wait_recv()

            pltpu.make_async_copy(W.at[layer, b], wall.at[layer, b], wsem.at[layer, b]).start()

        keep(0, layer, X, xs)
        for third in range(3):
            ready(QKV + third)

            def columns(c, _, third=third):
                cols = pl.ds(pl.multiple_of(c * 256, 256), 256)
                joined = dot(X[layer], W[layer, QKV + third, :, cols]) + SM[layer, B_QKV + third, :, cols]
                if third == 2:
                    QK[layer, third, :, cols] = joined.astype(BF16)
                else:
                    parts = []
                    for h in range(2):
                        t = joined[:, h * 128 : (h + 1) * 128]
                        parts.append((t * TAB[0] + swap_halves(t) * TAB[1]).astype(BF16))
                    QK[layer, third, :, cols] = jnp.concatenate(parts, axis=1)
                return 0

            lax.fori_loop(0, 3, columns, 0)
        keep(1, layer, QK, qkvs)

        def pair(hp, _):
            lanes = pl.ds(pl.multiple_of(hp * 128, 128), 128)
            q2 = QK[layer, 0, :, lanes]
            k2 = QK[layer, 1, :, lanes]
            v_t = QK[layer, 2, :, lanes].T
            low = low_lanes(k2.shape)
            outs = []
            for h in range(2):
                k_one = jnp.where(low if h == 0 else ~low, k2, jnp.zeros_like(k2))
                s = dot_t(k_one, q2) * SCORE + BIAS[...]
                peak = jnp.max(s, axis=0, keepdims=True)
                p = jnp.exp2(s - peak)
                total = jnp.sum(p, axis=0, keepdims=True)
                LSE[layer, hp, h : h + 1, :] = peak + jnp.log(total) * LOG2E
                outs.append(dot(v_t[h * HEAD : (h + 1) * HEAD], p.astype(BF16)) * (1.0 / total))
            ATT[layer, :, lanes] = jnp.concatenate(outs, axis=0).T.astype(BF16)
            return 0

        lax.fori_loop(0, PAIRS, pair, 0)
        keep(2, layer, LSE, lses)
        keep(3, layer, ATT, atts)
        ready(OUT)

        def norm_rows(r):
            mean = jnp.mean(r, axis=1, keepdims=True)
            centered = r - mean
            scale = lax.rsqrt(jnp.mean(centered * centered, axis=1, keepdims=True) + EPSILON)
            return centered * scale, scale

        def first_norm(c, _):
            rows = pl.ds(pl.multiple_of(c * 256, 256), 256)
            r = X[layer, rows, :].astype(F32) + dot(ATT[layer, rows, :], W[layer, OUT]) + SM[layer, B_OUT]
            n, scale = norm_rows(r)
            N1[layer, rows, :] = n.astype(BF16)
            RS[layer, 0, rows, :] = jnp.broadcast_to(scale, (256, 128))
            y = n * SM[layer, G_ATTN] + SM[layer, B_ATTN]
            NB[layer, rows, :] = y.astype(BF16)
            ACC[rows, :] = y + SM[layer, B_DOWN]
            return 0

        lax.fori_loop(0, tokens // 256, first_norm, 0)
        keep(4, layer, N1, n1s)
        keep(5, layer, NB, nbs)

        def ffn(f, _):
            ready(2 * f + 1)

            for c in range(3):
                cols = slice(c * 256, (c + 1) * 256)
                u = dot(NB[layer], W[layer, 2 * f + 1, :, cols]) + SM[layer, B_IN + f, :, cols]
                U[layer, f, :, cols] = u.astype(BF16)
                ACT[:, cols] = (0.5 * u * (1.0 + gelu_parts(u)[1])).astype(BF16)
            ready(2 * f)
            for c in range(3):
                cols = slice(c * 256, (c + 1) * 256)
                ACC[:, cols] += dot(ACT[...], W[layer, 2 * f, :, cols])
            return 0

        lax.fori_loop(0, CHUNKS, ffn, 0)
        keep(6, layer, U, us)

        def second_norm(c, _):
            rows = pl.ds(pl.multiple_of(c * 256, 256), 256)
            n, scale = norm_rows(ACC[rows, :])
            N2[layer, rows, :] = n.astype(BF16)
            RS[layer, 1, rows, :] = jnp.broadcast_to(scale, (256, 128))
            X[layer + 1, rows, :] = (n * SM[layer, G_FFN] + SM[layer, B_FFN]).astype(BF16)
            return 0

        lax.fori_loop(0, tokens // 256, second_norm, 0)
        keep(7, layer, N2, n2s)
        keep(8, layer, RS, rss)

        @pl.when(layer == sec)
        def _():
            pltpu.make_async_copy(X.at[layer + 1], acts.at[sec], asem.at[0]).start()

        @pl.when(layer != sec)
        def _():
            pltpu.make_async_remote_copy(
                X.at[layer + 1], acts.at[sec], asem.at[1], asem.at[2], device_id=peer, device_id_type=MESH
            ).start()

        return 0

    lax.fori_loop(0, 2, layer_step, 0)

    table_out.wait()
    bias_out.wait()
    small_out.wait()

    def finish(layer, _):
        for k, (src, dst) in enumerate(
            ((X, xs), (QK, qkvs), (LSE, lses), (ATT, atts), (N1, n1s), (NB, nbs), (U, us), (N2, n2s), (RS, rss))
        ):
            pltpu.make_async_copy(src.at[layer], dst.at[layer], stash.at[layer, k]).wait()
        for b in range(BLOCKS):
            pltpu.make_async_copy(W.at[layer, b], wall.at[layer, b], wsem.at[layer, b]).wait()
        return 0

    lax.fori_loop(0, 2, finish, 0)
    for b in range(BLOCKS):
        peer_copy(b).wait_send()
    pltpu.make_async_copy(X.at[1], acts.at[sec], asem.at[0]).wait()
    last = pltpu.make_async_remote_copy(
        X.at[1], acts.at[sec], asem.at[1], asem.at[2], device_id=peer, device_id_type=MESH
    )
    last.wait_send()
    last.wait_recv()


class Blocks:
    def __init__(self, G, RB, ST, peer_buf, outs, sems, dp, rep, dp_size, rep_size):
        self.G, self.RB, self.ST, self.peer_buf, self.outs = G, RB, ST, peer_buf, outs
        self.send, self.recv, self.load, self.out, self.peer_recv, self.peer_send, self.sync = sems
        self.dp, self.rep, self.n, self.rep_size = dp, rep, dp_size, rep_size
        self.line = dp_size == 4 and rep_size == 4
        self.ring = RB.shape[0]
        self.triples = 2 * BLOCKS // 3
        self.plans = {}
        self.steps = None
        for kind in (0, 1):
            self.steps = len(self.plan(jnp.int32(0), kind, jnp.int32(kind))) + 2
        assert self.steps - 1 < 2 * self.ring or self.ring >= self.triples

    def view(self, job, start, size):
        rows = pl.ds(pl.multiple_of(start, 16), size)
        cols = pl.ds(pl.multiple_of(job % 2 * HALF, 128), HALF)
        return self.G.at[job // 2, rows, cols]

    def landing(self, job, start, size):
        typ = job % 3
        return self.RB.at[job // 3 % self.ring, typ, pl.ds(pl.multiple_of(start, 16), size), :]

    def copy(self, job, k, src, dst, device):
        return pltpu.make_async_remote_copy(
            src, dst, self.send.at[job, k], self.recv.at[job, k], device_id=device, device_id_type=MESH
        )

    def add(self, job, start, place, size):
        step = 96 if size % 96 == 0 else 48
        g = self.view(job, start, size)
        r = self.landing(job, place, size)

        def body(i, _):
            rows = pl.ds(pl.multiple_of(i * step, 16), step)
            g[rows, :] = g[rows, :] + r[rows, :]
            return 0

        lax.fori_loop(0, size // step, body, 0)

    def move(self, job, start, place, size):
        g = self.view(job, start, size)
        r = self.landing(job, place, size)

        def body(i, _):
            rows = pl.ds(pl.multiple_of(i * 48, 16), 48)
            g[rows, :] = r[rows, :]
            return 0

        lax.fori_loop(0, size // 48, body, 0)

    def plan(self, job, kind, typ):
        self.sem_at = 0
        self.sync_at = 0
        self.place_at = 0
        if self.line:
            bits = [("rep", typ - 1), ("rep", 2 - typ)] if kind else [("rep", 0), ("rep", 1)]
            stages = bits + ["line"] if kind else ["line"] + bits
        else:
            stages = [("rep", b) for b in range(self.rep_size.bit_length() - 1)]
            stages += [("dp", b) for b in range(self.n.bit_length() - 1)]
        sizes, size = [], D
        for stage in stages:
            if stage == "line":
                size //= self.n
                sizes.append(size)
            elif self.halves(size):
                size //= 2
                sizes.append(size)
        start, size, cuts = jnp.int32(0), D, 0
        down, up = [], []
        for stage in stages:
            if stage == "line":
                cuts += 1
                start, size, a, b = self.line_stage(job, start, size, cuts == len(sizes))
            elif self.halves(size):
                cuts += 1
                start, size, a, b = self.pair_stage(job, start, size, *stage, cuts == len(sizes))
            else:
                a, b = self.swap_stage(job, start, size, *stage), []
            down = down + a
            up = b + up
        assert self.sem_at <= self.send.shape[1] and self.place_at <= self.RB.shape[2]
        assert self.sync_at <= self.sync.shape[1]
        return down + up

    @staticmethod
    def halves(size):
        return size // 2 % 48 == 0

    def take(self, sems, rows, syncs=0):
        k, place, y = self.sem_at, self.place_at, self.sync_at
        self.sem_at += sems
        self.place_at += rows
        self.sync_at += syncs
        return k, place, y

    def signal(self, job, y, device):
        pl.semaphore_signal(self.sync.at[job, y], inc=1, device_id=device, device_id_type=MESH)

    def swap_stage(self, job, start, size, axis, bit):
        index = self.rep if axis == "rep" else self.dp
        device = {axis: index ^ (1 << bit)}
        k, place, _ = self.take(1, size)

        def swap():
            return self.copy(job, k, self.view(job, start, size), self.landing(job, place, size), device)

        def finish():
            swap().wait()
            self.add(job, start, place, size)

        return [(lambda: swap().start(), finish, None, None)]

    def pair_stage(self, job, start, size, axis, bit, last):
        index = self.rep if axis == "rep" else self.dp
        mine = (index >> bit) & 1
        device = {axis: index ^ (1 << bit)}
        half = size // 2
        kept, given = start + mine * half, start + (1 - mine) * half
        k, place, y = self.take(2, 2 * half if last else half, 0 if last else 1)

        def down():
            return self.copy(job, k, self.view(job, given, half), self.landing(job, place, half), device)

        def up():
            there = self.landing(job, place + half, half) if last else self.view(job, kept, half)
            return self.copy(job, k + 1, self.view(job, kept, half), there, device)

        def finish_down():
            down().wait_recv()
            self.add(job, kept, place, half)

        def late():
            down().wait_send()
            if not last:
                self.signal(job, y, device)

        def start_up():
            if not last:
                pl.semaphore_wait(self.sync.at[job, y], 1)
            up().start()

        def finish_up():
            up().wait_recv()
            if last:
                down().wait_send()
                self.move(job, given, place + half, half)

        return (
            kept,
            half,
            [(lambda: down().start(), finish_down, None if last else late, None)],
            [(start_up, finish_up, None, lambda: up().wait_send())],
        )

    def line_stage(self, job, start, size, last):
        n, i = self.n, self.dp
        shard = size // n
        base, place, y = self.take(4 * (n - 1), (2 * n + 1 if last else n + 1) * shard, 0 if last else 2)
        right = {"dp": jnp.minimum(i + 1, n - 1)}
        left = {"dp": jnp.maximum(i - 1, 0)}

        def part(j):
            return self.view(job, start + j * shard, shard)

        def op(s, k, going_up):
            if going_up:
                send_r, send_l, take_r, take_l = i - s, i + s, i - 1 - s, i + 1 + s
                ok_sr, ok_sl = (i <= n - 2) & (send_r >= 0), (i >= 1) & (send_l <= n - 1)
                ok_tr, ok_tl = (i >= 1) & (take_r >= 0), (i <= n - 2) & (take_l <= n - 1)
            else:
                send_r, send_l, take_r, take_l = n - 1 - s + i, s + i - n + 1, n - 2 - s + i, s + i - n + 2
                ok_sr, ok_sl = (i <= n - 2) & (i <= s), (i >= 1) & (i >= n - 1 - s)
                ok_tr, ok_tl = (i >= 1) & (i - 1 <= s), (i <= n - 2) & (i >= n - 2 - s)

            def there(j, from_right):
                if going_up:
                    return self.landing(job, place + (n + 1 + j) * shard, shard) if last else part(j)
                slot = n if from_right and s == n - 2 else j
                return self.landing(job, place + slot * shard, shard)

            def to_right(j):
                return self.copy(job, k, part(j), there(j, False), right)

            def to_left(j):
                return self.copy(job, k + 1, part(j), there(j, True), left)

            def begin():
                if going_up and not last and s == 0:
                    pl.when(i >= 1)(lambda: pl.semaphore_wait(self.sync.at[job, y], 1))
                    pl.when(i <= n - 2)(lambda: pl.semaphore_wait(self.sync.at[job, y + 1], 1))
                pl.when(ok_sr)(lambda: to_right(send_r).start())
                pl.when(ok_sl)(lambda: to_left(send_l).start())

            def drain():
                pl.when(ok_sr)(lambda: to_right(send_r).wait_send())
                pl.when(ok_sl)(lambda: to_left(send_l).wait_send())

            def finish():
                def took(copy, j, slot):
                    copy.wait_recv()
                    if not going_up:
                        self.add(job, start + j * shard, place + slot * shard, shard)
                    elif last:
                        self.move(job, start + j * shard, place + (n + 1 + j) * shard, shard)

                if going_up and last and s == 0:
                    for one in down:
                        one[4]()
                pl.when(ok_tr)(lambda: took(to_right(take_r), take_r, take_r))
                pl.when(ok_tl)(lambda: took(to_left(take_l), take_l, n if s == n - 2 else take_l))

            def late():
                for one in down:
                    one[4]()
                pl.when(i <= n - 2)(lambda: self.signal(job, y, right))
                pl.when(i >= 1)(lambda: self.signal(job, y + 1, left))

            acked = not going_up and not last and s == n - 2
            return begin, finish, late if acked else None, drain if going_up else None, drain

        down = [op(s, base + 2 * s, False) for s in range(n - 1)]
        up = [op(s, base + 2 * (n - 1 + s), True) for s in range(n - 1)]
        return start + i * shard, shard, [one[:4] for one in down], [one[:4] for one in up]

    def peer_block(self, b):
        peer = {"section": 1 - lax.axis_index("section")}
        return pltpu.make_async_remote_copy(
            self.G.at[BLOCKS + b % 3],
            self.peer_buf.at[b],
            self.peer_send.at[b],
            self.peer_recv.at[b],
            device_id=peer,
            device_id_type=MESH,
        )

    def fetch(self, job):
        cols = pl.ds(pl.multiple_of(job % 2 * HALF, 128), HALF)
        return pltpu.make_async_copy(self.peer_buf.at[job // 2, :, cols], self.ST.at[job % 3], self.load.at[job % 3])

    def output(self, job):
        grad_q, grad_o, grad_i, grad_d = self.outs
        b, half = job // 2, pl.multiple_of(job % 2 * HALF, 128)
        src = self.G.at[b, :, pl.ds(half, HALF)]

        def to(dst):
            copy = pltpu.make_async_copy(src, dst, self.out.at[job])
            copy.start()

        pl.when((b < OUT) & (b % 2 == 0))(
            lambda: to(grad_d.at[pl.ds(pl.multiple_of(b // 2 % CHUNKS * D, D), D), pl.ds(half, HALF)])
        )
        pl.when((b < OUT) & (b % 2 == 1))(
            lambda: to(grad_i.at[:, pl.ds(pl.multiple_of(b // 2 % CHUNKS * D + half, 128), HALF)])
        )
        pl.when(b == OUT)(lambda: to(grad_o.at[:, pl.ds(half, HALF)]))
        pl.when(b > OUT)(
            lambda: to(grad_q.at[:, pl.ds(pl.multiple_of(jnp.maximum(b - QKV, 0) * D + half, 128), HALF)])
        )

    def step(self, triple, k, kind, typ):
        job = 3 * triple + typ
        if k == 0:

            @pl.when(job % 2 == 0)
            def _():
                self.peer_block(job // 2).wait_recv()

            self.fetch(job).start()
            return
        ops = self.plan(job, kind, typ)
        if k == 1:
            self.fetch(job).wait()
            g = self.view(job, 0, D)
            stage = self.ST.at[typ]

            def body(i, _):
                rows = pl.ds(pl.multiple_of(i * 96, 96), 96)
                g[rows, :] = g[rows, :] + stage[rows, :]
                return 0

            lax.fori_loop(0, D // 96, body, 0)
        else:
            ops[k - 2][1]()
        if k - 1 < len(ops):
            ops[k - 1][0]()
        if k >= 3 and ops[k - 3][2] is not None:
            ops[k - 3][2]()
        if k - 1 == len(ops):
            for op in ops:
                if op[3] is not None:
                    op[3]()
            self.output(job)

    def slot(self, t):
        for k in reversed(range(self.steps)):
            triple = (t - k) >> 1

            @pl.when((((t - k) & 1) == 0) & (t >= k) & (triple < self.triples))
            def _(k=k, triple=triple):
                self.step(triple, k, 0, jnp.int32(0))

                def rest(typ, _):
                    self.step(triple, k, 1, typ)
                    return 0

                lax.fori_loop(1, 3, rest, 0)

    @property
    def slots(self):
        return 2 * (self.triples - 1) + self.steps


CALLS = 9


def backward_kernel(
    dp_size, rep_size,
    cot, segc, wall, xs, qkvs, lses, atts, n1s, nbs, us, n2s, rss, tabs, biases, smalls,
    grad_q, grad_o, grad_i, grad_d, grad_small, ing, peer_buf,
    G, RB, ST, WR, UP, N2, NB, DB, DJ, N1, ATT, QK, U, TA, TN, DN, TAB, BIAS, RS, LSE, SM, SG, SB, SP,
    wsem, lsem, usem, send, recv, load, out, peer_send, peer_recv, gsem, ssend, srecv, sync,
):
    sec = lax.axis_index("section")
    dp = lax.axis_index("dp")
    rep = lax.axis_index("rep")
    peer = {"section": 1 - sec}
    tokens = UP.shape[0]
    sums = Blocks(
        G, RB, ST, peer_buf, (grad_q, grad_o, grad_i, grad_d),
        (send, recv, load, out, peer_recv, peer_send, sync), dp, rep, dp_size, rep_size,
    )

    def weight(seq):
        layer, b = 1 - seq // BLOCKS, seq % BLOCKS
        return pltpu.make_async_copy(wall.at[layer, b], WR.at[b % 4], wsem.at[b % 4])

    def u_copy(layer, f):
        return pltpu.make_async_copy(us.at[layer, f], U.at[f % 2], usem.at[f % 2])

    def loads(layer):
        return (
            pltpu.make_async_copy(n2s.at[layer], N2, lsem.at[0]),
            pltpu.make_async_copy(nbs.at[layer], NB, lsem.at[1]),
            pltpu.make_async_copy(n1s.at[layer], N1, lsem.at[2]),
            pltpu.make_async_copy(atts.at[layer], ATT, lsem.at[3]),
            pltpu.make_async_copy(qkvs.at[layer], QK, lsem.at[4]),
            pltpu.make_async_copy(rss.at[layer], RS, lsem.at[5]),
            pltpu.make_async_copy(lses.at[layer], LSE, lsem.at[6]),
            pltpu.make_async_copy(xs.at[layer], N2, lsem.at[7]),
        )

    first = (
        pltpu.make_async_copy(cot.at[sec], UP, lsem.at[8]),
        pltpu.make_async_copy(smalls, SM, lsem.at[9]),
        pltpu.make_async_copy(tabs, TAB, lsem.at[10]),
        pltpu.make_async_copy(biases, BIAS, lsem.at[11]),
    )
    for copy in first:
        copy.start()

    barrier = pltpu.get_barrier_semaphore()
    partners = [(peer, None)]
    partners += [({"rep": rep ^ (1 << b)}, None) for b in range(rep_size.bit_length() - 1)]
    partners += [({"dp": dp ^ (1 << b)}, None) for b in range(dp_size.bit_length() - 1)]
    if sums.line:
        partners += [({"dp": jnp.minimum(dp + 1, dp_size - 1)}, dp < dp_size - 1)]
        partners += [({"dp": jnp.maximum(dp - 1, 0)}, dp > 0)]
    count = 0
    for device, valid in partners:

        def greet(device=device):
            pl.semaphore_signal(barrier, inc=1, device_id=device, device_id_type=MESH)

        if valid is None:
            greet()
            count = count + 1
        else:
            pl.when(valid)(greet)
            count = count + jnp.where(valid, 1, 0)
    pl.semaphore_wait(barrier, count)

    for seq in range(4):
        weight(seq).start()
    real = jnp.where(segc[...] < SLOT // MINLEN, 1.0, 0.0).astype(F32)

    def in_copies(layer):
        mine = pltpu.make_async_copy(UP, ing.at[sec], gsem.at[0])
        theirs = pltpu.make_async_remote_copy(
            UP, ing.at[sec], gsem.at[1], gsem.at[2], device_id=peer, device_id_type=MESH
        )
        return mine, theirs

    def layer_step(li, _):
        layer = 1 - li
        copies = loads(layer)
        for copy in copies[:7]:
            copy.start()
        u_copy(layer, 0).start()
        u_copy(layer, 1).start()

        def target(b):
            return jnp.where(layer == sec, b, BLOCKS + b % 3)

        def slot(s):
            sums.slot((li - (1 - sec)) * CALLS + s)

        def before_block(b):
            @pl.when((layer != sec) & (b >= 3))
            def _():
                sums.peer_block(b - 3).wait_send()

        def after_block(b):
            @pl.when(layer != sec)
            def _():
                sums.peer_block(b).start()

        def outer(lhs_t, rhs, b):
            before_block(b)
            t = target(b)

            def columns(c, _):
                cols = pl.ds(pl.multiple_of(c * 256, 256), 256)
                G[t, :, cols] = dot(lhs_t[...], rhs[:, cols]).astype(BF16)
                return 0

            lax.fori_loop(0, 3, columns, 0)
            after_block(b)

        @pl.when(li == 0)
        def _():
            for copy in first:
                copy.wait()
            UP[...] = (UP[...].astype(F32) * real).astype(BF16)

        copies[0].wait()
        copies[5].wait()

        def norm_back(grad, n, gain, scale):
            a = grad * gain
            m1 = jnp.mean(a, axis=1, keepdims=True)
            m2 = jnp.mean(a * n, axis=1, keepdims=True)
            return (a - m1 - n * m2) * scale

        def rows_sum(value):
            return jnp.sum(value, axis=0, keepdims=True)

        for row in (G_FFN, B_FFN, B_DOWN, G_ATTN, B_ATTN, B_OUT):
            SG[layer, row] = jnp.zeros((1, D), F32)
        for row in (13, 14, 15):
            SG[layer, row] = jnp.zeros((1, D), F32)

        def second_norm(c, _):
            rows = pl.ds(pl.multiple_of(c * 256, 256), 256)
            up = UP[rows, :].astype(F32)
            n = N2[rows, :].astype(F32)
            scale = RS[1, rows, 0:1]
            g = norm_back(up, n, SM[layer, G_FFN], scale)
            DN[rows, :] = g
            DB[rows, :] = g.astype(BF16)
            SG[layer, G_FFN] += rows_sum(up * n)
            SG[layer, B_FFN] += rows_sum(up)
            SG[layer, B_DOWN] += rows_sum(g)
            return 0

        lax.fori_loop(0, tokens // 256, second_norm, 0)
        copies[7].start()
        copies[1].wait()
        TN[...] = NB[...].T

        def ffn(f, _):
            u_copy(layer, f).wait()
            weight(li * BLOCKS + 2 * f).wait()
            weight(li * BLOCKS + 2 * f + 1).wait()
            down, up = WR.at[2 * f % 4], WR.at[(2 * f + 1) % 4]
            for c in range(3):
                cols = slice(c * 256, (c + 1) * 256)
                u = U[f % 2, :, cols].astype(F32)
                square, t = gelu_parts(u)
                lift = 1.0 + t
                DJ[1, :, cols] = (0.5 * u * lift).astype(BF16)
                slope = 0.5 * lift * (1.0 + u * (1.0 - t) * (GELU_A * (1.0 + 3.0 * GELU_B * square)))
                grad = dot_t(DB[...], down[cols, :]) * slope
                SG[layer, B_IN + f, :, cols] = rows_sum(grad)
                DJ[0, :, cols] = grad.astype(BF16)
            TA[...] = DJ[1].T
            outer(TA, DB, 2 * f)
            outer(TN, DJ.at[0], 2 * f + 1)
            for c in range(3):
                cols = slice(c * 256, (c + 1) * 256)
                DN[:, cols] += dot_t(DJ[0], up[cols, :])
            weight(li * BLOCKS + 2 * f + 4).start()
            weight(li * BLOCKS + 2 * f + 5).start()
            pl.when(f + 2 < CHUNKS)(lambda: u_copy(layer, f + 2).start())
            slot(f)
            return 0

        lax.fori_loop(0, CHUNKS, ffn, 0)
        copies[2].wait()

        def first_norm(c, _):
            rows = pl.ds(pl.multiple_of(c * 256, 256), 256)
            up = DN[rows, :]
            n = N1[rows, :].astype(F32)
            g = norm_back(up, n, SM[layer, G_ATTN], RS[0, rows, 0:1])
            DN[rows, :] = g
            DB[rows, :] = g.astype(BF16)
            SG[layer, G_ATTN] += rows_sum(up * n)
            SG[layer, B_ATTN] += rows_sum(up)
            SG[layer, B_OUT] += rows_sum(g)
            return 0

        lax.fori_loop(0, tokens // 256, first_norm, 0)
        copies[3].wait()
        TA[...] = ATT[...].T
        outer(TA, DB, OUT)
        weight(li * BLOCKS + OUT).wait()
        w_out = WR.at[OUT % 4]
        for c in range(3):
            cols = slice(c * 256, (c + 1) * 256)
            NB[:, cols] = dot_t(DB[...], w_out[cols, :]).astype(BF16)
        pl.when(li == 0)(lambda: weight(BLOCKS).start())
        slot(CHUNKS)
        copies[4].wait()
        copies[6].wait()

        def pair(hp, _):
            lanes = pl.ds(pl.multiple_of(hp * 128, 128), 128)
            q2 = QK[0, :, lanes]
            k2 = QK[1, :, lanes]
            v2 = QK[2, :, lanes]
            o2 = NB[:, lanes]
            low = low_lanes(k2.shape)
            k_t = k2.T
            zero = jnp.zeros_like(k2)
            grads_q, grads_k, grads_v = [], [], []
            for h in range(2):
                mask = low if h == 0 else ~low
                s = dot_t(jnp.where(mask, k2, zero), q2) * SCORE + BIAS[...]
                p = jnp.exp2(s - LSE[hp, h : h + 1, :])
                dprob = dot_t(jnp.where(mask, v2, zero), o2)
                inner = jnp.sum(p * dprob, axis=0, keepdims=True)
                ds = (p * (dprob - inner)).astype(BF16)
                grads_v.append(dot(p.astype(BF16), o2))
                grads_k.append(dot(ds, q2))
                grads_q.append(dot(k_t[h * HEAD : (h + 1) * HEAD], ds))
            scale = 1.0 / math.sqrt(HEAD)
            gq = jnp.concatenate(grads_q, axis=0).T * scale
            gk = jnp.where(low, grads_k[0], grads_k[1]) * scale
            gv = jnp.where(low, grads_v[0], grads_v[1])
            cos, sin = TAB[0], TAB[1]
            gq = gq * cos - swap_halves(gq) * sin
            gk = gk * cos - swap_halves(gk) * sin
            for third, g in enumerate((gq, gk, gv)):
                DJ[third, :, lanes] = g.astype(BF16)
                SG[layer, B_QKV + third, :, lanes] = rows_sum(g)
            pl.when(hp % 2 == 1)(lambda: slot(CHUNKS + 1 + hp // 2))
            return 0

        lax.fori_loop(0, PAIRS, pair, 0)
        copies[7].wait()
        TN[...] = N2[...].T

        def third_step(third, _):
            outer(TN, DJ.at[third], QKV + third)
            weight(li * BLOCKS + QKV + third).wait()
            w = WR.at[(QKV + third) % 4]
            for c in range(3):
                cols = slice(c * 256, (c + 1) * 256)
                DN[:, cols] += dot_t(DJ[third], w[cols, :])
            pl.when(li == 0)(lambda: weight(BLOCKS + 1 + third).start())
            return 0

        lax.fori_loop(0, 3, third_step, 0)

        @pl.when(layer != sec)
        def _():
            for b in range(BLOCKS - 3, BLOCKS):
                sums.peer_block(b).wait_send()

        mine, theirs = in_copies(layer)
        @pl.when(li == 1)
        def _():
            pl.when(sec == 1)(lambda: mine.wait())
            pl.when(sec == 0)(lambda: theirs.wait_send())

        UP[...] = DN[...].astype(BF16)
        pl.when(layer == sec)(lambda: mine.start())
        pl.when(layer != sec)(lambda: theirs.start())
        slot(CALLS - 1)
        return 0

    lax.fori_loop(0, 2, layer_step, 0)

    small_partners = [peer] + [device for device, valid in partners[1:] if valid is None]

    def small_copy(m):
        src = SG.at[1 - sec] if m == 0 else SP.at[m - 1]
        return pltpu.make_async_remote_copy(
            src, SB.at[m], ssend.at[m], srecv.at[m], device_id=small_partners[m], device_id_type=MESH
        )

    small_copy(0).start()

    def small_step(m):
        small_copy(m).wait_recv()
        SP[m] = (SG[sec] if m == 0 else SP[m - 1]) + SB[m]
        if m + 1 < len(small_partners):
            small_copy(m + 1).start()

    rounds = max(sums.slots - CALLS, len(small_partners))

    def final(i, _):
        sums.slot((1 + sec) * CALLS + i)
        for m in range(len(small_partners)):
            pl.when(i == m)(functools.partial(small_step, m))
        return 0

    lax.fori_loop(0, rounds, final, 0)
    for m in range(len(small_partners)):
        small_copy(m).wait_send()
    small_out = pltpu.make_async_copy(SP.at[len(small_partners) - 1], grad_small, ssend.at[0])
    small_out.start()

    def out_wait(job, _):
        pltpu.make_async_copy(G.at[0, :, pl.ds(0, HALF)], grad_o.at[:, pl.ds(0, HALF)], out.at[job]).wait()
        return 0

    lax.fori_loop(0, 2 * BLOCKS, out_wait, 0)
    small_out.wait()
    mine, theirs = in_copies(0)
    pl.when(sec == 0)(lambda: mine.wait())
    pl.when(sec == 1)(lambda: theirs.wait_send())
    theirs.wait_recv()


def per_device(
    dp_size, rep_size, inputs, segments, cotangent, w_qkv, b_qkv, w_out, b_out, g_attn, b_attn, w_in, b_in, w_down,
    b_down, g_ffn, b_ffn,
):
    sec = lax.axis_index("section")
    tokens = inputs.shape[1]
    own = lax.dynamic_index_in_dim(segments, sec, 0, keepdims=False)
    rows = [b_qkv.reshape(3, D), b_out, g_attn, b_attn, b_in.reshape(CHUNKS, D), b_down, g_ffn, b_ffn]
    small = jnp.concatenate([row.astype(F32) for row in rows] + [jnp.zeros((3, D), F32)], axis=0)
    small = small.reshape(SMALL, 1, D)
    anywhere = pl.BlockSpec(memory_space=pl.ANY)
    in_vmem = pl.BlockSpec(memory_space=pltpu.VMEM)

    def shape(*dims, dtype=BF16):
        return jax.ShapeDtypeStruct(dims, dtype)

    def mem(*dims, dtype=BF16):
        return pltpu.VMEM(dims, dtype)

    dma = pltpu.SemaphoreType.DMA
    stash = pl.pallas_call(
        forward_kernel,
        out_shape=(
            shape(2, BLOCKS, D, D),
            shape(2, tokens, D),
            shape(2, 3, tokens, D),
            shape(2, PAIRS, 8, tokens, dtype=F32),
            shape(2, tokens, D),
            shape(2, tokens, D),
            shape(2, tokens, D),
            shape(2, CHUNKS, tokens, D),
            shape(2, tokens, D),
            shape(2, 2, tokens, 128, dtype=F32),
            shape(2, tokens, 128, dtype=F32),
            shape(tokens, tokens, dtype=F32),
            shape(2, tokens, D),
            shape(2, SMALL, 1, D, dtype=F32),
        ),
        in_specs=[anywhere, in_vmem, in_vmem] + [anywhere] * 4 + [in_vmem],
        out_specs=(anywhere,) * 14,
        scratch_shapes=[
            mem(2, BLOCKS, D, D),
            mem(2, SMALL, 1, D, dtype=F32),
            mem(3, tokens, D),
            mem(2, 3, tokens, D),
            mem(2, PAIRS, 8, tokens, dtype=F32),
            mem(2, tokens, D),
            mem(2, tokens, D),
            mem(2, tokens, D),
            mem(2, CHUNKS, tokens, D),
            mem(2, tokens, D),
            mem(2, 2, tokens, 128, dtype=F32),
            mem(2, tokens, 128, dtype=F32),
            mem(tokens, tokens, dtype=F32),
            mem(tokens, D, dtype=F32),
            mem(tokens, D),
            dma((BLOCKS,)),
            dma((BLOCKS,)),
            dma((BLOCKS,)),
            dma((6,)),
            dma((2, BLOCKS)),
            dma((2, 9)),
            dma((3,)),
        ],
        compiler_params=pltpu.CompilerParams(collective_id=0, has_side_effects=True, vmem_limit_bytes=VMEM_LIMIT),
        name="forward",
    )(inputs, own.reshape(1, tokens), own.reshape(tokens, 1), w_qkv, w_out, w_in, w_down, small)
    (wall, xs, qkvs, lses, atts, n1s, nbs, us, n2s, rss, tabs, biases, acts, smalls) = stash

    line = dp_size == 4 and rep_size == 4
    bits = dp_size.bit_length() + rep_size.bit_length() - 2
    ring = 6 if line else 8
    landing = 1152 if line else 912
    sems = 16
    out = pl.pallas_call(
        functools.partial(backward_kernel, dp_size, rep_size),
        out_shape=(
            shape(D, 3 * D),
            shape(D, D),
            shape(D, CHUNKS * D),
            shape(CHUNKS * D, D),
            shape(SMALL, 1, D, dtype=F32),
            shape(2, tokens, D),
            shape(BLOCKS, D, D),
        ),
        in_specs=[anywhere, in_vmem] + [anywhere] * 13,
        out_specs=(anywhere,) * 7,
        scratch_shapes=[
            mem(BLOCKS + 3, D, D),
            mem(ring, 3, landing, HALF),
            mem(3, D, HALF),
            mem(4, D, D),
            mem(tokens, D),
            mem(tokens, D),
            mem(tokens, D),
            mem(tokens, D),
            mem(3, tokens, D),
            mem(tokens, D),
            mem(tokens, D),
            mem(3, tokens, D),
            mem(2, tokens, D),
            mem(D, tokens),
            mem(D, tokens),
            mem(tokens, D, dtype=F32),
            mem(2, tokens, 128, dtype=F32),
            mem(tokens, tokens, dtype=F32),
            mem(2, tokens, 128, dtype=F32),
            mem(PAIRS, 8, tokens, dtype=F32),
            mem(2, SMALL, 1, D, dtype=F32),
            mem(2, SMALL, 1, D, dtype=F32),
            mem(bits + 1, SMALL, 1, D, dtype=F32),
            mem(bits + 1, SMALL, 1, D, dtype=F32),
            dma((4,)),
            dma((12,)),
            dma((2,)),
            dma((2 * BLOCKS, sems)),
            dma((2 * BLOCKS, sems)),
            dma((3,)),
            dma((2 * BLOCKS,)),
            dma((BLOCKS,)),
            dma((BLOCKS,)),
            dma((3,)),
            dma((bits + 1,)),
            dma((bits + 1,)),
            pltpu.SemaphoreType.REGULAR((2 * BLOCKS, 4)),
        ],
        compiler_params=pltpu.CompilerParams(collective_id=1, has_side_effects=True, vmem_limit_bytes=VMEM_LIMIT),
        name="backward",
    )(cotangent, own.reshape(tokens, 1), wall, xs, qkvs, lses, atts, n1s, nbs, us, n2s, rss, tabs, biases, smalls)
    grad_q, grad_o, grad_i, grad_d, grad_small, ing, _ = out
    grads = grad_small.reshape(SMALL, D)

    def row(start, count=1):
        return grads[start : start + count].reshape(1, count * D)

    return (
        acts[None],
        ing[None],
        grad_q.astype(F32)[None],
        row(B_QKV, 3),
        grad_o.astype(F32)[None],
        row(B_OUT),
        row(G_ATTN),
        row(B_ATTN),
        grad_i.astype(F32)[None],
        row(B_IN, CHUNKS),
        grad_d.astype(F32)[None],
        row(B_DOWN),
        row(G_FFN),
        row(B_FFN),
    )


def solution(mesh):
    tokens = ("dp", "rep")
    weight, vector = P("section", None, None), P("section", None)
    weights = (weight, vector, weight, vector, vector, vector, weight, vector, weight, vector, vector, vector)
    activations = P("section", None, tokens, None)
    return jax.shard_map(
        functools.partial(per_device, mesh.shape["dp"], mesh.shape["rep"]),
        mesh=mesh,
        in_specs=(P(None, tokens, None), P(None, tokens), P(None, tokens, None), *weights),
        out_specs=(activations, activations, *weights),
        check_vma=False,
    )
```

time: 1410 us -> 340 us (0.24)
  waiting for transfers between devices: 539 us -> 0 us
  matrix products: 461 us -> 0 us
  Pallas kernels: 0 us -> 309 us
  blocking collectives: 149 us -> 0 us
  other arithmetic: 120 us -> 18 us
  local copies, waits for them, and re-layouts: 102 us -> 12 us
  between operations: 21.7 us -> 0.73 us
    reduce_scatter x4 -> x0, waiting for transfers between devices: 467 us -> none  [the longest x1 176 us: per_device(): lax.psum_scatter(running_ffn[0], ('dp', 'rep'), scatter_dimension=0, tile...]
    dot_general x69 -> x0, matrix products: 427 us -> none  [the longest x3 64.2 us: backward_attn(): jnp.einsum('hqk,qhd->khd', grad_scores, queries, preferred_element_type=j...]
    pallas_call x0 -> x2, Pallas kernels: none -> 309 us  [the longest x1 259 us: per_device(): pl.pallas_call(functools.partial(backward_kernel, dp_size, rep_size), out...]
    unnamed x2 -> x0, blocking collectives: 149 us -> none
    all_gather x4 -> x0, waiting for transfers between devices: 71.2 us -> none  [the longest x1 71.2 us: per_device(): lax.all_gather(running[8].astype(jnp.bfloat16), ('dp', 'rep'), axis=0, ti...]
    add x7 -> x0, local copies, waits for them, and re-layouts: 37.4 us -> none  [the longest x6 36.6 us: forward_layer(): jnp.dot(source, w_qkv, preferred_element_type=jnp.float32)]
    reduce_sum x36 -> x0, other arithmetic: 35.2 us -> none  [the longest x3 11.2 us: forward_layer(): row_total = jnp.sum(exponent, axis=-1, keepdims=True)]
    sub x3 -> x0, matrix products: 33.7 us -> none  [forward_layer(): exponent = jnp.exp(scores - peak_score)]
  transfers between devices with their start and end apart: 12 -> 0, of which waited for: 6 -> 0; matrix products, arithmetic and copies ran while one was open for 21% -> 0% of each run, Pallas kernels for 0% -> 0%
where the time goes in v1:
time: 340 us
  Pallas kernels  309 us (91%)
  other arithmetic  18 us (5%)
  local copies, waits for them, and re-layouts  12 us (4%)
    pallas_call x1, Pallas kernels, per_device(): pl.pallas_call(functools.partial(backward_kernel, dp_size, rep_size), out...  259 us
    pallas_call x1, Pallas kernels, per_device(): pl.pallas_call(forward_kernel, out_shape=(shape(2, BLOCKS, D, D), shape(2...  50.1 us

profile of v1, /device:TPU:0, one launch (start us, length us, event | category | flops | bytes accessed | tf_op | source)
XLA Modules:
  0.0 339.6 jit_solution(16860595421598472268)
XLA Ops:
  0.6 0.0 copy-start
  0.7 0.7 copy-done
  1.3 0.6 constant_dynamic-slice_fusion.segr
  1.9 0.7 convert_reduce_fusion.1
  2.7 0.7 convert_reduce_fusion
  3.4 1.6 concatenate.3
  5.0 0.7 reshape.61.small
  5.7 0.9 copy.29.segc
  6.6 50.1 %forward.1 = (bf16[2,12,768,768]{3,2,1,0:T(8,128)(2,1)}, bf16[2,512,768]{2,1,0:T(8,128)(2,1)}, bf16[2,3,512,768]{3,2,1,0:T(8,128)(2,1)}, f32[2,6,8,512]{3,2,1,0:...) custom-call(bf16[2,512,768]{2,1,0:T(8,128)(2,1)} %inp.1, ...), custom_call_target="tpu_custom_call" | custom-call | tf_op jit(solution)/shard_map/forward/pallas_call | solution.py:932
  56.6 258.8 %backward.1 = (bf16[768,2304]{1,0:T(8,128)(2,1)}, bf16[768,768]{1,0:T(8,128)(2,1)}, bf16[768,3072]{1,0:T(8,128)(2,1)}, bf16[3072,768]{1,0:T(8,128)(2,1)}, f32[16...) custom-call(bf16[2,512,768]{2,1,0:T(8,128)(2,1)} %cot.1, s32[512,1]{1,0:T(8,128)} %copy.29.segc, ...), custom_call_target="tpu_custom_call" | custom-call | tf_op jit(solution)/shard_map/backward/pallas_call | solution.py:986
  315.4 0.0 copy-start.3
  315.4 1.5 slice.44
  316.9 1.3 slice.51
  318.2 1.3 slice_bitcast_fusion
  319.5 2.8 bitcast_convert_fusion.3
  322.3 4.1 %bitcast_convert_fusion.2 = f32[1,768,2304]{2,1,0:T(8,128)} fusion(bf16[768,2304]{1,0:T(8,128)(2,1)S(1)} %copy-done.3), kind=kLoop, calls=%fused_computation.2 | loop fusion | flops 1769472 | bytes 10616832 | tf_op jit(solution)/shard_map/broadcast_in_dim | solution.py:1050
  326.4 0.4 copy-done.2
  326.9 5.0 %bitcast_convert_fusion.1 = f32[1,768,3072]{2,1,0:T(8,128)} fusion(bf16[768,3072]{1,0:T(8,128)(2,1)S(1)} %copy-done.2), kind=kLoop, calls=%fused_computation.1 | loop fusion | flops 2359296 | bytes 14155776 | tf_op jit(solution)/shard_map/broadcast_in_dim | solution.py:1056
  331.9 0.0 slice-done
  331.9 0.0 copy-start.1
  331.9 4.5 %bitcast_convert_fusion = f32[1,3072,768]{2,1,0:T(8,128)} fusion(bf16[3072,768]{1,0:T(8,128)(2,1)S(1)} %bitcast.31), kind=kLoop, calls=%fused_computation | loop fusion | flops 2359296 | bytes 14155776 | tf_op jit(solution)/shard_map/broadcast_in_dim | solution.py:1058
  336.4 1.1 copy.33
  337.6 0.8 copy-done.5
  338.4 1.1 copy.34
  (14 shorter events, 0.0 us)
Async XLA Ops:
  0.6 0.7 copy-start
  315.4 6.9 %copy-start.3 = (bf16[768,2304]{1,0:T(8,128)(2,1)S(1)}, bf16[768,2304]{1,0:T(8,128)(2,1)}, u32[]{:S(2)}) copy-start(bf16[768,2304]{1,0:T(8,128)(2,1)} %get-tuple-element.49) | copy-start | bytes 10616836
  322.3 4.5 %copy-start.2 = (bf16[768,3072]{1,0:T(8,128)(2,1)S(1)}, bf16[768,3072]{1,0:T(8,128)(2,1)}, u32[]{:S(2)}) copy-start(bf16[768,3072]{1,0:T(8,128)(2,1)} %get-tuple-element.52) | copy-start | bytes 14155780
  322.3 9.6 %slice-start = ((s8[4718592]{0:T(1024)(128)(4,1)}), s8[4194304]{0:T(1024)(128)(4,1)S(1)}, s32[]{:S(2)}) async-start(s8[4718592]{0:T(1024)(128)(4,1)} %bitcast.30), calls=%async_computation | async-start | bytes 8388608
  326.9 5.1 %slice-start.1 = ((s8[4718592]{0:T(1024)(128)(4,1)}), s8[524288]{0:T(1024)(128)(4,1)S(1)}, s32[]{:S(2)}) async-start(s8[4718592]{0:T(1024)(128)(4,1)} %bitcast.30), calls=%async_computation.1 | async-start | bytes 1048576
  331.9 4.5 %copy-start.4 = (bf16[2,512,768]{2,1,0:T(8,128)(2,1)S(1)}, bf16[2,512,768]{2,1,0:T(8,128)(2,1)}, u32[]{:S(2)}) copy-start(bf16[2,512,768]{2,1,0:T(8,128)(2,1)} %get-tuple-element.34) | copy-start | bytes 4718596
  331.9 7.6 %copy-start.1 = (s32[2,512]{1,0:T(2,128)S(1)}, s32[2,512]{1,0:T(2,128)}, u32[]{:S(2)}) copy-start(s32[2,512]{1,0:T(2,128)} %param.16) | copy-start | bytes 12292
  336.4 2.0 copy-start.5

commit v2 on v1

--- a/solution.py
+++ b/solution.py
@@ -27,7 +27,38 @@
 SCORE = LOG2E / math.sqrt(HEAD)
 GELU_A = math.sqrt(2.0 / math.pi)
 GELU_B = 0.044715
-HALF = D // 2
+THIRD = D // 3
+OWN = BLOCKS // 2
+CALLS = 18
+FINAL = 2 * CALLS
+TABLE = (
+    (1, 2, 5, 8, 11, 14, 17, 20, 23, 26, 29, 32),
+    (3, 4, 7, 10, 13, 16, 19, 22, 25, 28, 31, 34),
+    (5, 6, 9, 12, 15, 18, 21, 24, 27, 30, 33, 36),
+    (7, 8, 11, 14, 17, 20, 23, 26, 29, 32, 35, 37),
+    (15, 16, 19, 22, 25, 28, 31, 34, 36, 37, 38, 39),
+    (17, 18, 21, 24, 27, 30, 33, 36, 37, 38, 39, 40),
+    (19, 20, 23, 26, 29, 32, 35, 37, 38, 39, 40, 41),
+    (21, 22, 25, 28, 31, 34, 36, 38, 39, 40, 41, 42),
+    (23, 24, 27, 30, 33, 36, 37, 39, 40, 41, 42, 43),
+    (25, 26, 29, 32, 35, 37, 38, 40, 41, 42, 43, 44),
+    (33, 34, 36, 37, 38, 39, 40, 41, 42, 43, 44, 45),
+    (35, 36, 37, 38, 39, 40, 41, 42, 43, 44, 45, 46),
+)
+
+
+def timetable(steps):
+    ready = [CALLS * li + at for li in range(2) for at in (1, 3, 5, 7, 15, 17)]
+    table = []
+    for o, first in enumerate(ready):
+        times = []
+        for k in range(steps):
+            t = max(first, times[-1] + 1 if k else 0, table[-1][k] + 1 if o else 0)
+            times.append(t)
+        table.append(times)
+    return table
+
+
 MESH = pl.DeviceIdType.MESH
 F32 = jnp.float32
 BF16 = jnp.bfloat16
@@ -42,6 +73,10 @@
     return lax.dot_general(a, b, (((1,), (1,)), ((), ())), preferred_element_type=F32)
 
 
+def dot_tn(a, b):
+    return lax.dot_general(a, b, (((0,), (0,)), ((), ())), preferred_element_type=F32)
+
+
 def swap_halves(t):
     lane = lax.broadcasted_iota(jnp.int32, t.shape, 1)
     return jnp.where(lane % HEAD < HEAD // 2, pltpu.roll(t, 96, 1), pltpu.roll(t, 32, 1))
@@ -49,6 +84,11 @@
 
 def low_lanes(shape):
     return lax.broadcasted_iota(jnp.int32, shape, 1) < HEAD
+
+
+def own_segments(segs, sec):
+    row = jnp.where(sec == 0, segs[0:1, :], segs[1:2, :]).astype(F32)
+    return row, jnp.broadcast_to(row, (128, row.shape[1])).T[:, 0:1]
 
 
 def gelu_parts(u):
@@ -58,7 +98,7 @@
 
 
 def forward_kernel(
-    inp, segr, segc, wq, wo, wi, wd, small,
+    inp, segs, wq, wo, wi, wd, bq, bo, ga, ba, bi, bd, gf, bf,
     wall, xs, qkvs, lses, atts, n1s, nbs, us, n2s, rss, tabs, biases, acts, smalls,
     W, SM, X, QK, LSE, ATT, N1, NB, U, N2, RS, TAB, BIAS, ACC, ACT,
     osem, rsend, rrecv, ssem, wsem, stash, asem,
@@ -91,20 +131,23 @@
     barrier = pltpu.get_barrier_semaphore()
     pl.semaphore_signal(barrier, inc=1, device_id=peer, device_id_type=MESH)
     pl.semaphore_wait(barrier, 1)
+    for row, ref in ((B_QKV, bq), (B_OUT, bo), (G_ATTN, ga), (B_ATTN, ba), (B_IN, bi), (B_DOWN, bd), (G_FFN, gf), (B_FFN, bf)):
+        for i in range(ref.shape[1] // D):
+            SM[sec, row + i] = ref[0:1, i * D : (i + 1) * D].astype(F32)
+    for row in range(B_FFN + 1, SMALL):
+        SM[sec, row] = jnp.zeros((1, D), F32)
     small_copy = pltpu.make_async_remote_copy(
-        small, SM.at[sec], ssem.at[1], ssem.at[2], device_id=peer, device_id_type=MESH
+        SM.at[sec], SM.at[sec], ssem.at[1], ssem.at[2], device_id=peer, device_id_type=MESH
     )
     small_copy.start()
     for b in SEND_ORDER:
         peer_copy(b).start()
     for b in SEND_ORDER[4:]:
         own_copy(b).start()
-    SM[sec] = small[...]
 
     row_at = lax.broadcasted_iota(jnp.int32, (tokens, tokens), 0)
     col_at = lax.broadcasted_iota(jnp.int32, (tokens, tokens), 1)
-    seg_col = segc[...]
-    seg_row = segr[...]
+    seg_row, seg_col = own_segments(segs, sec)
     same = seg_col == seg_row
     position = jnp.sum(jnp.where(same & (col_at < row_at), 1.0, 0.0), axis=1, keepdims=True)
     allowed = (same & (seg_col < SLOT // MINLEN)) | (row_at == col_at)
@@ -145,8 +188,8 @@
         for third in range(3):
             ready(QKV + third)
 
-            def columns(c, _, third=third):
-                cols = pl.ds(pl.multiple_of(c * 256, 256), 256)
+            for c in range(3):
+                cols = slice(c * 256, (c + 1) * 256)
                 joined = dot(X[layer], W[layer, QKV + third, :, cols]) + SM[layer, B_QKV + third, :, cols]
                 if third == 2:
                     QK[layer, third, :, cols] = joined.astype(BF16)
@@ -156,9 +199,6 @@
                         t = joined[:, h * 128 : (h + 1) * 128]
                         parts.append((t * TAB[0] + swap_halves(t) * TAB[1]).astype(BF16))
                     QK[layer, third, :, cols] = jnp.concatenate(parts, axis=1)
-                return 0
-
-            lax.fori_loop(0, 3, columns, 0)
         keep(1, layer, QK, qkvs)
 
         def pair(hp, _):
@@ -275,86 +315,77 @@
 class Blocks:
     def __init__(self, G, RB, ST, peer_buf, outs, sems, dp, rep, dp_size, rep_size):
         self.G, self.RB, self.ST, self.peer_buf, self.outs = G, RB, ST, peer_buf, outs
-        self.send, self.recv, self.load, self.out, self.peer_recv, self.peer_send, self.sync = sems
-        self.dp, self.rep, self.n, self.rep_size = dp, rep, dp_size, rep_size
+        (self.send, self.recv, self.load, self.out, self.out_recv, self.peer_recv, self.peer_send, self.sync) = sems
+        self.sec, self.dp, self.rep, self.n, self.rep_size = lax.axis_index("section"), dp, rep, dp_size, rep_size
         self.line = dp_size == 4 and rep_size == 4
         self.ring = RB.shape[0]
-        self.triples = 2 * BLOCKS // 3
-        self.plans = {}
-        self.steps = None
         for kind in (0, 1):
             self.steps = len(self.plan(jnp.int32(0), kind, jnp.int32(kind))) + 2
-        assert self.steps - 1 < 2 * self.ring or self.ring >= self.triples
+        self.table = TABLE if self.steps == len(TABLE[0]) else timetable(self.steps)
 
     def view(self, job, start, size):
+        block, typ = job
         rows = pl.ds(pl.multiple_of(start, 16), size)
-        cols = pl.ds(pl.multiple_of(job % 2 * HALF, 128), HALF)
-        return self.G.at[job // 2, rows, cols]
+        cols = pl.ds(pl.multiple_of(typ * THIRD, 128), THIRD)
+        return self.G.at[block, rows, cols]
 
     def landing(self, job, start, size):
-        typ = job % 3
-        return self.RB.at[job // 3 % self.ring, typ, pl.ds(pl.multiple_of(start, 16), size), :]
-
-    def copy(self, job, k, src, dst, device):
+        block, typ = job
+        return self.RB.at[block % self.ring, typ, pl.ds(pl.multiple_of(start, 16), size), :]
+
+    def copy(self, job, k, src, dst, device, side=0):
+        block, typ = job
+        slot = block % self.ring * 3 + typ
         return pltpu.make_async_remote_copy(
-            src, dst, self.send.at[job, k], self.recv.at[job, k], device_id=device, device_id_type=MESH
+            src, dst, self.send.at[slot, side], self.recv.at[slot, k], device_id=device, device_id_type=MESH
         )
 
-    def add(self, job, start, place, size):
+    def combine(self, job, start, place, size, add):
         step = 96 if size % 96 == 0 else 48
         g = self.view(job, start, size)
         r = self.landing(job, place, size)
 
         def body(i, _):
             rows = pl.ds(pl.multiple_of(i * step, 16), step)
-            g[rows, :] = g[rows, :] + r[rows, :]
+            g[rows, :] = g[rows, :] + r[rows, :] if add else r[rows, :]
             return 0
 
         lax.fori_loop(0, size // step, body, 0)
 
-    def move(self, job, start, place, size):
-        g = self.view(job, start, size)
-        r = self.landing(job, place, size)
-
-        def body(i, _):
-            rows = pl.ds(pl.multiple_of(i * 48, 16), 48)
-            g[rows, :] = r[rows, :]
-            return 0
-
-        lax.fori_loop(0, size // 48, body, 0)
-
     def plan(self, job, kind, typ):
+        if not isinstance(job, tuple):
+            job = (job, typ)
         self.sem_at = 0
         self.sync_at = 0
         self.place_at = 0
         if self.line:
-            bits = [("rep", typ - 1), ("rep", 2 - typ)] if kind else [("rep", 0), ("rep", 1)]
+            bits = [("rep", typ - 1), ("rep", 2 - typ)] if kind else [("rep", job[0] & 1), ("rep", 1 - (job[0] & 1))]
             stages = bits + ["line"] if kind else ["line"] + bits
         else:
             stages = [("rep", b) for b in range(self.rep_size.bit_length() - 1)]
             stages += [("dp", b) for b in range(self.n.bit_length() - 1)]
-        sizes, size = [], D
+        total, size = 0, D
         for stage in stages:
             if stage == "line":
                 size //= self.n
-                sizes.append(size)
+                total += 1
             elif self.halves(size):
                 size //= 2
-                sizes.append(size)
+                total += 1
         start, size, cuts = jnp.int32(0), D, 0
         down, up = [], []
         for stage in stages:
             if stage == "line":
                 cuts += 1
-                start, size, a, b = self.line_stage(job, start, size, cuts == len(sizes))
+                start, size, a, b = self.line_stage(job, start, size, cuts == total)
             elif self.halves(size):
                 cuts += 1
-                start, size, a, b = self.pair_stage(job, start, size, *stage, cuts == len(sizes))
+                start, size, a, b = self.pair_stage(job, start, size, *stage, cuts == total)
             else:
                 a, b = self.swap_stage(job, start, size, *stage), []
             down = down + a
             up = b + up
-        assert self.sem_at <= self.send.shape[1] and self.place_at <= self.RB.shape[2]
+        assert self.sem_at <= self.recv.shape[1] and self.place_at <= self.RB.shape[2]
         assert self.sync_at <= self.sync.shape[1]
         return down + up
 
@@ -369,8 +400,11 @@
         self.sync_at += syncs
         return k, place, y
 
+    def ack(self, job, y):
+        return self.sync.at[job[0] % self.ring * 3 + job[1], y]
+
     def signal(self, job, y, device):
-        pl.semaphore_signal(self.sync.at[job, y], inc=1, device_id=device, device_id_type=MESH)
+        pl.semaphore_signal(self.ack(job, y), inc=1, device_id=device, device_id_type=MESH)
 
     def swap_stage(self, job, start, size, axis, bit):
         index = self.rep if axis == "rep" else self.dp
@@ -382,9 +416,9 @@
 
         def finish():
             swap().wait()
-            self.add(job, start, place, size)
-
-        return [(lambda: swap().start(), finish, None, None)]
+            self.combine(job, start, place, size, True)
+
+        return [(lambda: swap().start(), finish)]
 
     def pair_stage(self, job, start, size, axis, bit, last):
         index = self.rep if axis == "rep" else self.dp
@@ -392,53 +426,47 @@
         device = {axis: index ^ (1 << bit)}
         half = size // 2
         kept, given = start + mine * half, start + (1 - mine) * half
-        k, place, y = self.take(2, 2 * half if last else half, 0 if last else 1)
+        k, place, y = self.take(2 if last else 1, 2 * half if last else half, 0 if last else 1)
 
         def down():
             return self.copy(job, k, self.view(job, given, half), self.landing(job, place, half), device)
 
         def up():
             there = self.landing(job, place + half, half) if last else self.view(job, kept, half)
-            return self.copy(job, k + 1, self.view(job, kept, half), there, device)
+            return self.copy(job, k + 1 if last else k, self.view(job, kept, half), there, device)
 
         def finish_down():
             down().wait_recv()
-            self.add(job, kept, place, half)
-
-        def late():
+            self.combine(job, kept, place, half, True)
             down().wait_send()
             if not last:
                 self.signal(job, y, device)
 
         def start_up():
             if not last:
-                pl.semaphore_wait(self.sync.at[job, y], 1)
+                pl.semaphore_wait(self.ack(job, y), 1)
             up().start()
 
         def finish_up():
-            up().wait_recv()
+            up().wait()
             if last:
-                down().wait_send()
-                self.move(job, given, place + half, half)
-
-        return (
-            kept,
-            half,
-            [(lambda: down().start(), finish_down, None if last else late, None)],
-            [(start_up, finish_up, None, lambda: up().wait_send())],
-        )
+                self.combine(job, given, place + half, half, False)
+
+        return kept, half, [(lambda: down().start(), finish_down)], [(start_up, finish_up)]
 
     def line_stage(self, job, start, size, last):
         n, i = self.n, self.dp
         shard = size // n
-        base, place, y = self.take(4 * (n - 1), (2 * n + 1 if last else n + 1) * shard, 0 if last else 2)
+        per_side = n if last else n - 1
+        base, place, y = self.take(2 * per_side, (2 * n + 1 if last else n + 1) * shard, 0 if last else 2)
         right = {"dp": jnp.minimum(i + 1, n - 1)}
         left = {"dp": jnp.maximum(i - 1, 0)}
 
         def part(j):
             return self.view(job, start + j * shard, shard)
 
-        def op(s, k, going_up):
+        def op(s, going_up):
+            k = base + 2 * (s + 1 if going_up and last and s == n - 2 else s)
             if going_up:
                 send_r, send_l, take_r, take_l = i - s, i + s, i - 1 - s, i + 1 + s
                 ok_sr, ok_sl = (i <= n - 2) & (send_r >= 0), (i >= 1) & (send_l <= n - 1)
@@ -455,146 +483,144 @@
                 return self.landing(job, place + slot * shard, shard)
 
             def to_right(j):
-                return self.copy(job, k, part(j), there(j, False), right)
+                return self.copy(job, k, part(j), there(j, False), right, 0)
 
             def to_left(j):
-                return self.copy(job, k + 1, part(j), there(j, True), left)
+                return self.copy(job, k + 1, part(j), there(j, True), left, 1)
 
             def begin():
                 if going_up and not last and s == 0:
-                    pl.when(i >= 1)(lambda: pl.semaphore_wait(self.sync.at[job, y], 1))
-                    pl.when(i <= n - 2)(lambda: pl.semaphore_wait(self.sync.at[job, y + 1], 1))
+                    pl.when(i >= 1)(lambda: pl.semaphore_wait(self.ack(job, y), 1))
+                    pl.when(i <= n - 2)(lambda: pl.semaphore_wait(self.ack(job, y + 1), 1))
                 pl.when(ok_sr)(lambda: to_right(send_r).start())
                 pl.when(ok_sl)(lambda: to_left(send_l).start())
-
-            def drain():
-                pl.when(ok_sr)(lambda: to_right(send_r).wait_send())
-                pl.when(ok_sl)(lambda: to_left(send_l).wait_send())
 
             def finish():
                 def took(copy, j, slot):
                     copy.wait_recv()
                     if not going_up:
-                        self.add(job, start + j * shard, place + slot * shard, shard)
+                        self.combine(job, start + j * shard, place + slot * shard, shard, True)
                     elif last:
-                        self.move(job, start + j * shard, place + (n + 1 + j) * shard, shard)
-
-                if going_up and last and s == 0:
-                    for one in down:
-                        one[4]()
+                        self.combine(job, start + j * shard, place + (n + 1 + j) * shard, shard, False)
+
                 pl.when(ok_tr)(lambda: took(to_right(take_r), take_r, take_r))
                 pl.when(ok_tl)(lambda: took(to_left(take_l), take_l, n if s == n - 2 else take_l))
-
-            def late():
-                for one in down:
-                    one[4]()
-                pl.when(i <= n - 2)(lambda: self.signal(job, y, right))
-                pl.when(i >= 1)(lambda: self.signal(job, y + 1, left))
-
-            acked = not going_up and not last and s == n - 2
-            return begin, finish, late if acked else None, drain if going_up else None, drain
-
-        down = [op(s, base + 2 * s, False) for s in range(n - 1)]
-        up = [op(s, base + 2 * (n - 1 + s), True) for s in range(n - 1)]
-        return start + i * shard, shard, [one[:4] for one in down], [one[:4] for one in up]
-
-    def peer_block(self, b):
-        peer = {"section": 1 - lax.axis_index("section")}
+                pl.when(ok_sr)(lambda: to_right(send_r).wait_send())
+                pl.when(ok_sl)(lambda: to_left(send_l).wait_send())
+                if not going_up and not last and s == n - 2:
+                    pl.when(i <= n - 2)(lambda: self.signal(job, y, right))
+                    pl.when(i >= 1)(lambda: self.signal(job, y + 1, left))
+
+            return begin, finish
+
+        return start + i * shard, shard, [op(s, False) for s in range(n - 1)], [op(s, True) for s in range(n - 1)]
+
+    def peer_block(self, o):
         return pltpu.make_async_remote_copy(
-            self.G.at[BLOCKS + b % 3],
-            self.peer_buf.at[b],
-            self.peer_send.at[b],
-            self.peer_recv.at[b],
-            device_id=peer,
+            self.G.at[BLOCKS + o % 2],
+            self.peer_buf.at[o],
+            self.peer_send.at[o],
+            self.peer_recv.at[o],
+            device_id={"section": 1 - self.sec},
             device_id_type=MESH,
         )
 
-    def fetch(self, job):
-        cols = pl.ds(pl.multiple_of(job % 2 * HALF, 128), HALF)
-        return pltpu.make_async_copy(self.peer_buf.at[job // 2, :, cols], self.ST.at[job % 3], self.load.at[job % 3])
-
-    def output(self, job):
+    def fetch(self, o):
+        return pltpu.make_async_copy(self.peer_buf.at[o], self.ST, self.load.at[0])
+
+    def result(self, o, dst, remote):
+        if remote:
+            return pltpu.make_async_remote_copy(
+                self.G.at[o],
+                dst,
+                self.out.at[o],
+                self.out_recv.at[o],
+                device_id={"section": 1 - self.sec},
+                device_id_type=MESH,
+            )
+        return pltpu.make_async_copy(self.G.at[o], dst, self.out.at[o])
+
+    def output(self, o):
         grad_q, grad_o, grad_i, grad_d = self.outs
-        b, half = job // 2, pl.multiple_of(job % 2 * HALF, 128)
-        src = self.G.at[b, :, pl.ds(half, HALF)]
+        layer, b = 1 - o // OWN, o % OWN * 2 + self.sec
 
         def to(dst):
-            copy = pltpu.make_async_copy(src, dst, self.out.at[job])
-            copy.start()
-
-        pl.when((b < OUT) & (b % 2 == 0))(
-            lambda: to(grad_d.at[pl.ds(pl.multiple_of(b // 2 % CHUNKS * D, D), D), pl.ds(half, HALF)])
-        )
-        pl.when((b < OUT) & (b % 2 == 1))(
-            lambda: to(grad_i.at[:, pl.ds(pl.multiple_of(b // 2 % CHUNKS * D + half, 128), HALF)])
-        )
-        pl.when(b == OUT)(lambda: to(grad_o.at[:, pl.ds(half, HALF)]))
-        pl.when(b > OUT)(
-            lambda: to(grad_q.at[:, pl.ds(pl.multiple_of(jnp.maximum(b - QKV, 0) * D + half, 128), HALF)])
-        )
-
-    def step(self, triple, k, kind, typ):
-        job = 3 * triple + typ
+            pl.when(layer == self.sec)(lambda: self.result(o, dst, False).start())
+            pl.when(layer != self.sec)(lambda: self.result(o, dst, True).start())
+
+        chunk = pl.ds(pl.multiple_of(b // 2 % CHUNKS * D, D), D)
+        third = pl.ds(pl.multiple_of(jnp.maximum(b - QKV, 0) * D, D), D)
+        pl.when((b < OUT) & (b % 2 == 0))(lambda: to(grad_d.at[chunk, :]))
+        pl.when((b < OUT) & (b % 2 == 1))(lambda: to(grad_i.at[:, chunk]))
+        pl.when(b == OUT)(lambda: to(grad_o))
+        pl.when(b > OUT)(lambda: to(grad_q.at[:, third]))
+
+    def wait_output(self, o):
+        grad_o = self.outs[1]
+        layer = 1 - o // OWN
+
+        @pl.when(layer == self.sec)
+        def _():
+            self.result(o, grad_o, False).wait()
+            self.result(o, grad_o, True).wait_recv()
+
+        @pl.when(layer != self.sec)
+        def _():
+            self.result(o, grad_o, True).wait_send()
+
+    def step(self, o, k):
         if k == 0:
-
-            @pl.when(job % 2 == 0)
-            def _():
-                self.peer_block(job // 2).wait_recv()
-
-            self.fetch(job).start()
+            self.peer_block(o).wait_recv()
+            self.fetch(o).start()
             return
-        ops = self.plan(job, kind, typ)
         if k == 1:
-            self.fetch(job).wait()
-            g = self.view(job, 0, D)
-            stage = self.ST.at[typ]
+            self.fetch(o).wait()
+            g, stage = self.G.at[o], self.ST
 
             def body(i, _):
-                rows = pl.ds(pl.multiple_of(i * 96, 96), 96)
+                rows = pl.ds(pl.multiple_of(i * 48, 48), 48)
                 g[rows, :] = g[rows, :] + stage[rows, :]
                 return 0
 
-            lax.fori_loop(0, D // 96, body, 0)
-        else:
-            ops[k - 2][1]()
-        if k - 1 < len(ops):
-            ops[k - 1][0]()
-        if k >= 3 and ops[k - 3][2] is not None:
-            ops[k - 3][2]()
-        if k - 1 == len(ops):
-            for op in ops:
-                if op[3] is not None:
-                    op[3]()
-            self.output(job)
+            lax.fori_loop(0, D // 48, body, 0)
+
+        def advance(kind, typ):
+            ops = self.plan((o, typ), kind, typ)
+            if k >= 2:
+                ops[k - 2][1]()
+            if k - 1 < len(ops):
+                ops[k - 1][0]()
+
+        advance(0, jnp.int32(0))
+
+        def rest(typ, _):
+            advance(1, typ)
+            return 0
+
+        lax.fori_loop(1, 3, rest, 0)
+        if k == self.steps - 1:
+            self.output(o)
 
     def slot(self, t):
         for k in reversed(range(self.steps)):
-            triple = (t - k) >> 1
-
-            @pl.when((((t - k) & 1) == 0) & (t >= k) & (triple < self.triples))
-            def _(k=k, triple=triple):
-                self.step(triple, k, 0, jnp.int32(0))
-
-                def rest(typ, _):
-                    self.step(triple, k, 1, typ)
-                    return 0
-
-                lax.fori_loop(1, 3, rest, 0)
+            o, valid = jnp.int32(0), False
+            for block, times in enumerate(self.table):
+                due = t == times[k]
+                o = jnp.where(due, block, o)
+                valid = valid | due
+            pl.when(valid)(functools.partial(self.step, o, k))
 
     @property
     def slots(self):
-        return 2 * (self.triples - 1) + self.steps
-
-
-CALLS = 9
+        return self.table[-1][-1] + 1
 
 
 def backward_kernel(
     dp_size, rep_size,
-    cot, segc, wall, xs, qkvs, lses, atts, n1s, nbs, us, n2s, rss, tabs, biases, smalls,
+    cot, segs, wall, xs, qkvs, lses, atts, n1s, nbs, us, n2s, rss, tabs, biases, smalls,
     grad_q, grad_o, grad_i, grad_d, grad_small, ing, peer_buf,
-    G, RB, ST, WR, UP, N2, NB, DB, DJ, N1, ATT, QK, U, TA, TN, DN, TAB, BIAS, RS, LSE, SM, SG, SB, SP,
-    wsem, lsem, usem, send, recv, load, out, peer_send, peer_recv, gsem, ssend, srecv, sync,
+    G, RB, ST, WR, UP, N2, NB, DB, DJ, N1, ATT, QK, U, DAT, DN, TAB, BIAS, RS, LSE, SM, SG, SB, SP,
+    wsem, lsem, usem, send, recv, load, out, out_recv, peer_send, peer_recv, gsem, ssend, srecv, sync,
 ):
     sec = lax.axis_index("section")
     dp = lax.axis_index("dp")
@@ -603,7 +629,7 @@
     tokens = UP.shape[0]
     sums = Blocks(
         G, RB, ST, peer_buf, (grad_q, grad_o, grad_i, grad_d),
-        (send, recv, load, out, peer_recv, peer_send, sync), dp, rep, dp_size, rep_size,
+        (send, recv, load, out, out_recv, peer_recv, peer_send, sync), dp, rep, dp_size, rep_size,
     )
 
     def weight(seq):
@@ -657,7 +683,7 @@
 
     for seq in range(4):
         weight(seq).start()
-    real = jnp.where(segc[...] < SLOT // MINLEN, 1.0, 0.0).astype(F32)
+    real = jnp.where(own_segments(segs, sec)[1] < SLOT // MINLEN, 1.0, 0.0).astype(F32)
 
     def in_copies(layer):
         mine = pltpu.make_async_copy(UP, ing.at[sec], gsem.at[0])
@@ -674,33 +700,23 @@
         u_copy(layer, 0).start()
         u_copy(layer, 1).start()
 
-        def target(b):
-            return jnp.where(layer == sec, b, BLOCKS + b % 3)
-
         def slot(s):
-            sums.slot((li - (1 - sec)) * CALLS + s)
-
-        def before_block(b):
-            @pl.when((layer != sec) & (b >= 3))
+            sums.slot(li * CALLS + s)
+
+        def outer(lhs, rhs, b):
+            o = li * OWN + b // 2
+            mine = b % 2 == sec
+
+            @pl.when(~mine & (o >= 2))
             def _():
-                sums.peer_block(b - 3).wait_send()
-
-        def after_block(b):
-            @pl.when(layer != sec)
-            def _():
-                sums.peer_block(b).start()
-
-        def outer(lhs_t, rhs, b):
-            before_block(b)
-            t = target(b)
-
-            def columns(c, _):
-                cols = pl.ds(pl.multiple_of(c * 256, 256), 256)
-                G[t, :, cols] = dot(lhs_t[...], rhs[:, cols]).astype(BF16)
-                return 0
-
-            lax.fori_loop(0, 3, columns, 0)
-            after_block(b)
+                sums.peer_block(o - 2).wait_send()
+
+            t = jnp.where(mine, o, BLOCKS + o % 2)
+            for c in range(3):
+                cols = slice(c * 256, (c + 1) * 256)
+                G[t, :, cols] = dot_tn(lhs[...], rhs[:, cols]).astype(BF16)
+
+            pl.when(~mine)(lambda: sums.peer_block(o).start())
 
         @pl.when(li == 0)
         def _():
@@ -741,7 +757,6 @@
         lax.fori_loop(0, tokens // 256, second_norm, 0)
         copies[7].start()
         copies[1].wait()
-        TN[...] = NB[...].T
 
         def ffn(f, _):
             u_copy(layer, f).wait()
@@ -758,16 +773,16 @@
                 grad = dot_t(DB[...], down[cols, :]) * slope
                 SG[layer, B_IN + f, :, cols] = rows_sum(grad)
                 DJ[0, :, cols] = grad.astype(BF16)
-            TA[...] = DJ[1].T
-            outer(TA, DB, 2 * f)
-            outer(TN, DJ.at[0], 2 * f + 1)
+            outer(DJ.at[1], DB, 2 * f)
+            slot(2 * f)
+            outer(NB, DJ.at[0], 2 * f + 1)
             for c in range(3):
                 cols = slice(c * 256, (c + 1) * 256)
                 DN[:, cols] += dot_t(DJ[0], up[cols, :])
             weight(li * BLOCKS + 2 * f + 4).start()
             weight(li * BLOCKS + 2 * f + 5).start()
             pl.when(f + 2 < CHUNKS)(lambda: u_copy(layer, f + 2).start())
-            slot(f)
+            slot(2 * f + 1)
             return 0
 
         lax.fori_loop(0, CHUNKS, ffn, 0)
@@ -787,15 +802,14 @@
 
         lax.fori_loop(0, tokens // 256, first_norm, 0)
         copies[3].wait()
-        TA[...] = ATT[...].T
-        outer(TA, DB, OUT)
+        outer(ATT, DB, OUT)
         weight(li * BLOCKS + OUT).wait()
         w_out = WR.at[OUT % 4]
         for c in range(3):
             cols = slice(c * 256, (c + 1) * 256)
-            NB[:, cols] = dot_t(DB[...], w_out[cols, :]).astype(BF16)
+            DAT[:, cols] = dot_t(DB[...], w_out[cols, :]).astype(BF16)
         pl.when(li == 0)(lambda: weight(BLOCKS).start())
-        slot(CHUNKS)
+        slot(2 * CHUNKS)
         copies[4].wait()
         copies[6].wait()
 
@@ -804,7 +818,7 @@
             q2 = QK[0, :, lanes]
             k2 = QK[1, :, lanes]
             v2 = QK[2, :, lanes]
-            o2 = NB[:, lanes]
+            o2 = DAT[:, lanes]
             low = low_lanes(k2.shape)
             k_t = k2.T
             zero = jnp.zeros_like(k2)
@@ -829,29 +843,24 @@
             for third, g in enumerate((gq, gk, gv)):
                 DJ[third, :, lanes] = g.astype(BF16)
                 SG[layer, B_QKV + third, :, lanes] = rows_sum(g)
-            pl.when(hp % 2 == 1)(lambda: slot(CHUNKS + 1 + hp // 2))
+            slot(2 * CHUNKS + 1 + hp)
             return 0
 
         lax.fori_loop(0, PAIRS, pair, 0)
         copies[7].wait()
-        TN[...] = N2[...].T
 
         def third_step(third, _):
-            outer(TN, DJ.at[third], QKV + third)
+            outer(N2, DJ.at[third], QKV + third)
             weight(li * BLOCKS + QKV + third).wait()
             w = WR.at[(QKV + third) % 4]
             for c in range(3):
                 cols = slice(c * 256, (c + 1) * 256)
                 DN[:, cols] += dot_t(DJ[third], w[cols, :])
             pl.when(li == 0)(lambda: weight(BLOCKS + 1 + third).start())
+            slot(CALLS - 3 + third)
             return 0
 
         lax.fori_loop(0, 3, third_step, 0)
-
-        @pl.when(layer != sec)
-        def _():
-            for b in range(BLOCKS - 3, BLOCKS):
-                sums.peer_block(b).wait_send()
 
         mine, theirs = in_copies(layer)
         @pl.when(li == 1)
@@ -862,7 +871,6 @@
         UP[...] = DN[...].astype(BF16)
         pl.when(layer == sec)(lambda: mine.start())
         pl.when(layer != sec)(lambda: theirs.start())
-        slot(CALLS - 1)
         return 0
 
     lax.fori_loop(0, 2, layer_step, 0)
@@ -883,10 +891,10 @@
         if m + 1 < len(small_partners):
             small_copy(m + 1).start()
 
-    rounds = max(sums.slots - CALLS, len(small_partners))
+    rounds = max(sums.slots - 2 * CALLS, len(small_partners))
 
     def final(i, _):
-        sums.slot((1 + sec) * CALLS + i)
+        sums.slot(2 * CALLS + i)
         for m in range(len(small_partners)):
             pl.when(i == m)(functools.partial(small_step, m))
         return 0
@@ -897,11 +905,14 @@
     small_out = pltpu.make_async_copy(SP.at[len(small_partners) - 1], grad_small, ssend.at[0])
     small_out.start()
 
-    def out_wait(job, _):
-        pltpu.make_async_copy(G.at[0, :, pl.ds(0, HALF)], grad_o.at[:, pl.ds(0, HALF)], out.at[job]).wait()
+    for o in (BLOCKS - 2, BLOCKS - 1):
+        sums.peer_block(o).wait_send()
+
+    def out_wait(o, _):
+        sums.wait_output(o)
         return 0
 
-    lax.fori_loop(0, 2 * BLOCKS, out_wait, 0)
+    lax.fori_loop(0, BLOCKS, out_wait, 0)
     small_out.wait()
     mine, theirs = in_copies(0)
     pl.when(sec == 0)(lambda: mine.wait())
@@ -909,16 +920,51 @@
     theirs.wait_recv()
 
 
+RING = 6
+ROWS = 256
+
+
+def convert_kernel(
+    grad_q, grad_o, grad_i, grad_d, small,
+    out_q, out_o, out_i, out_d, b_q, b_o, g_a, b_a, b_i, b_d, g_f, b_f,
+    LOW, HIGH, isem, osem,
+):
+    tiles = []
+    for src, dst in ((grad_q, out_q), (grad_o, out_o), (grad_i, out_i), (grad_d, out_d)):
+        for r in range(src.shape[0] // ROWS):
+            for c in range(src.shape[1] // D):
+                part = (pl.ds(r * ROWS, ROWS), pl.ds(c * D, D))
+                tiles.append((src.at[part], dst.at[0, part[0], part[1]]))
+    reads = [pltpu.make_async_copy(src, LOW.at[i % RING], isem.at[i % RING]) for i, (src, _) in enumerate(tiles)]
+    writes = [pltpu.make_async_copy(HIGH.at[i % RING], dst, osem.at[i % RING]) for i, (_, dst) in enumerate(tiles)]
+    for i in range(RING):
+        reads[i].start()
+    for row, ref in ((B_QKV, b_q), (B_OUT, b_o), (G_ATTN, g_a), (B_ATTN, b_a), (B_IN, b_i), (B_DOWN, b_d), (G_FFN, g_f), (B_FFN, b_f)):
+        for i in range(ref.shape[1] // D):
+            ref[0:1, i * D : (i + 1) * D] = small[row + i]
+    for i in range(len(tiles)):
+        reads[i].wait()
+        if i >= RING:
+            writes[i - RING].wait()
+
+        def body(r, _, at=i % RING):
+            rows = pl.ds(pl.multiple_of(r * 64, 64), 64)
+            HIGH[at, rows, :] = LOW[at, rows, :].astype(F32)
+            return 0
+
+        lax.fori_loop(0, ROWS // 64, body, 0)
+        writes[i].start()
+        if i + RING < len(tiles):
+            reads[i + RING].start()
+    for write in writes[len(tiles) - RING :]:
+        write.wait()
+
+
 def per_device(
     dp_size, rep_size, inputs, segments, cotangent, w_qkv, b_qkv, w_out, b_out, g_attn, b_attn, w_in, b_in, w_down,
     b_down, g_ffn, b_ffn,
 ):
-    sec = lax.axis_index("section")
     tokens = inputs.shape[1]
-    own = lax.dynamic_index_in_dim(segments, sec, 0, keepdims=False)
-    rows = [b_qkv.reshape(3, D), b_out, g_attn, b_attn, b_in.reshape(CHUNKS, D), b_down, g_ffn, b_ffn]
-    small = jnp.concatenate([row.astype(F32) for row in rows] + [jnp.zeros((3, D), F32)], axis=0)
-    small = small.reshape(SMALL, 1, D)
     anywhere = pl.BlockSpec(memory_space=pl.ANY)
     in_vmem = pl.BlockSpec(memory_space=pltpu.VMEM)
 
@@ -947,7 +993,7 @@
             shape(2, tokens, D),
             shape(2, SMALL, 1, D, dtype=F32),
         ),
-        in_specs=[anywhere, in_vmem, in_vmem] + [anywhere] * 4 + [in_vmem],
+        in_specs=[anywhere, in_vmem] + [anywhere] * 4 + [in_vmem] * 8,
         out_specs=(anywhere,) * 14,
         scratch_shapes=[
             mem(2, BLOCKS, D, D),
@@ -975,14 +1021,13 @@
         ],
         compiler_params=pltpu.CompilerParams(collective_id=0, has_side_effects=True, vmem_limit_bytes=VMEM_LIMIT),
         name="forward",
-    )(inputs, own.reshape(1, tokens), own.reshape(tokens, 1), w_qkv, w_out, w_in, w_down, small)
+    )(inputs, segments, w_qkv, w_out, w_in, w_down, b_qkv, b_out, g_attn, b_attn, b_in, b_down, g_ffn, b_ffn)
     (wall, xs, qkvs, lses, atts, n1s, nbs, us, n2s, rss, tabs, biases, acts, smalls) = stash
 
     line = dp_size == 4 and rep_size == 4
     bits = dp_size.bit_length() + rep_size.bit_length() - 2
-    ring = 6 if line else 8
+    ring = BLOCKS
     landing = 1152 if line else 912
-    sems = 16
     out = pl.pallas_call(
         functools.partial(backward_kernel, dp_size, rep_size),
         out_shape=(
@@ -997,9 +1042,9 @@
         in_specs=[anywhere, in_vmem] + [anywhere] * 13,
         out_specs=(anywhere,) * 7,
         scratch_shapes=[
-            mem(BLOCKS + 3, D, D),
-            mem(ring, 3, landing, HALF),
-            mem(3, D, HALF),
+            mem(BLOCKS + 2, D, D),
+            mem(ring, 3, landing, THIRD),
+            mem(D, D),
             mem(4, D, D),
             mem(tokens, D),
             mem(tokens, D),
@@ -1010,8 +1055,7 @@
             mem(tokens, D),
             mem(3, tokens, D),
             mem(2, tokens, D),
-            mem(D, tokens),
-            mem(D, tokens),
+            mem(tokens, D),
             mem(tokens, D, dtype=F32),
             mem(2, tokens, 128, dtype=F32),
             mem(tokens, tokens, dtype=F32),
@@ -1024,42 +1068,42 @@
             dma((4,)),
             dma((12,)),
             dma((2,)),
-            dma((2 * BLOCKS, sems)),
-            dma((2 * BLOCKS, sems)),
-            dma((3,)),
-            dma((2 * BLOCKS,)),
+            dma((3 * ring, 2)),
+            dma((3 * ring, 10)),
+            dma((1,)),
+            dma((BLOCKS,)),
+            dma((BLOCKS,)),
             dma((BLOCKS,)),
             dma((BLOCKS,)),
             dma((3,)),
             dma((bits + 1,)),
             dma((bits + 1,)),
-            pltpu.SemaphoreType.REGULAR((2 * BLOCKS, 4)),
+            pltpu.SemaphoreType.REGULAR((3 * ring, 3)),
         ],
         compiler_params=pltpu.CompilerParams(collective_id=1, has_side_effects=True, vmem_limit_bytes=VMEM_LIMIT),
         name="backward",
-    )(cotangent, own.reshape(tokens, 1), wall, xs, qkvs, lses, atts, n1s, nbs, us, n2s, rss, tabs, biases, smalls)
+    )(cotangent, segments, wall, xs, qkvs, lses, atts, n1s, nbs, us, n2s, rss, tabs, biases, smalls)
     grad_q, grad_o, grad_i, grad_d, grad_small, ing, _ = out
-    grads = grad_small.reshape(SMALL, D)
-
-    def row(start, count=1):
-        return grads[start : start + count].reshape(1, count * D)
-
-    return (
-        acts[None],
-        ing[None],
-        grad_q.astype(F32)[None],
-        row(B_QKV, 3),
-        grad_o.astype(F32)[None],
-        row(B_OUT),
-        row(G_ATTN),
-        row(B_ATTN),
-        grad_i.astype(F32)[None],
-        row(B_IN, CHUNKS),
-        grad_d.astype(F32)[None],
-        row(B_DOWN),
-        row(G_FFN),
-        row(B_FFN),
-    )
+    vectors = (3 * D, D, D, D, CHUNKS * D, D, D, D)
+    grads = pl.pallas_call(
+        convert_kernel,
+        out_shape=(
+            *(shape(1, *grad.shape, dtype=F32) for grad in (grad_q, grad_o, grad_i, grad_d)),
+            *(shape(1, size, dtype=F32) for size in vectors),
+        ),
+        in_specs=[anywhere] * 4 + [in_vmem],
+        out_specs=(anywhere,) * 4 + (in_vmem,) * 8,
+        scratch_shapes=[
+            mem(RING, ROWS, D),
+            mem(RING, ROWS, D, dtype=F32),
+            dma((RING,)),
+            dma((RING,)),
+        ],
+        compiler_params=pltpu.CompilerParams(vmem_limit_bytes=VMEM_LIMIT),
+        name="convert",
+    )(grad_q, grad_o, grad_i, grad_d, grad_small)
+    grad_q, grad_o, grad_i, grad_d, b_q, b_o, g_a, b_a, b_i, b_d, g_f, b_f = grads
+    return acts[None], ing[None], grad_q, b_q, grad_o, b_o, g_a, b_a, grad_i, b_i, grad_d, b_d, g_f, b_f
 
 
 def solution(mesh):

time: 340 us -> 305 us (0.90)
  other arithmetic: 18 us -> 0 us
  Pallas kernels: 309 us -> 300 us
  local copies, waits for them, and re-layouts: 12 us -> 3.1 us
    pallas_call x1, Pallas kernels: 259 us -> 236 us  [per_device(): pl.pallas_call(functools.partial(backward_kernel, dp_size, rep_size), out...]
    pallas_call x0 -> x1, Pallas kernels: none -> 16.6 us  [per_device(): pl.pallas_call(convert_kernel, out_shape=(*(shape(1, *grad.shape, dtype=F...]
    broadcast_in_dim x4 -> x0, other arithmetic: 16.5 us -> none  [the longest x1 5.05 us: per_device(): grad_i.astype(F32)[None]]
    slice x3 -> x0, local copies, waits for them, and re-layouts: 4.06 us -> none  [row(): return grads[start:start + count].reshape(1, count * D)]
where the time goes in v2:
time: 305 us; the launch traced here: 304 us
  Pallas kernels  300 us (98%)
  local copies, waits for them, and re-layouts  3.1 us (1%)
    pallas_call x1, Pallas kernels, per_device(): pl.pallas_call(functools.partial(backward_kernel, dp_size, rep_size), out...  236 us
    pallas_call x1, Pallas kernels, per_device(): pl.pallas_call(forward_kernel, out_shape=(shape(2, BLOCKS, D, D), shape(2...  47.8 us
    pallas_call x1, Pallas kernels, per_device(): pl.pallas_call(convert_kernel, out_shape=(*(shape(1, *grad.shape, dtype=F...  16.6 us

profile of v2, /device:TPU:0, one launch (start us, length us, event | category | flops | bytes accessed | tf_op | source)
XLA Modules:
  0.0 303.9 jit_solution(15274713248624156414)
XLA Ops:
  0.7 47.8 %forward.1 = (bf16[2,12,768,768]{3,2,1,0:T(8,128)(2,1)}, bf16[2,512,768]{2,1,0:T(8,128)(2,1)}, bf16[2,3,512,768]{3,2,1,0:T(8,128)(2,1)}, f32[2,6,8,512]{3,2,1,0:...) custom-call(bf16[2,512,768]{2,1,0:T(8,128)(2,1)} %inp.1, ...), custom_call_target="tpu_custom_call" | custom-call | tf_op jit(solution)/shard_map/forward/pallas_call | solution.py:978
  48.4 235.8 %backward.1 = (bf16[768,2304]{1,0:T(8,128)(2,1)}, bf16[768,768]{1,0:T(8,128)(2,1)}, bf16[768,3072]{1,0:T(8,128)(2,1)}, bf16[3072,768]{1,0:T(8,128)(2,1)}, f32[16...) custom-call(bf16[2,512,768]{2,1,0:T(8,128)(2,1)} %cot.1, s32[2,512]{1,0:T(2,128)} %segs.3, ...), custom_call_target="tpu_custom_call" | custom-call | tf_op jit(solution)/shard_map/backward/pallas_call | solution.py:1031
  284.2 0.0 copy-start
  284.3 16.6 %convert.1 = (f32[1,768,2304]{2,1,0:T(8,128)}, f32[1,768,768]{2,1,0:T(8,128)}, f32[1,768,3072]{2,1,0:T(8,128)}, f32[1,3072,768]{2,1,0:T(8,128)}, f32[1,2304]{1,0...) custom-call(bf16[768,2304]{1,0:T(8,128)(2,1)} %get-tuple-element.61., ...), custom_call_target="tpu_custom_call" | custom-call | tf_op jit(solution)/shard_map/convert/pallas_call | solution.py:1088
  300.8 0.0 copy-start.1
  300.8 0.0 copy-done
  300.8 1.1 copy.31
  302.0 0.8 copy-done.1
  302.8 1.1 copy.32
Async XLA Ops:
  284.2 16.6 %copy-start = (bf16[2,512,768]{2,1,0:T(8,128)(2,1)S(1)}, bf16[2,512,768]{2,1,0:T(8,128)(2,1)}, u32[]{:S(2)}) copy-start(bf16[2,512,768]{2,1,0:T(8,128)(2,1)} %get-tuple-element.46) | copy-start | bytes 4718596
  300.8 2.0 copy-start.1

commit v3 on v2

--- a/solution.py
+++ b/solution.py
@@ -32,16 +32,16 @@
 CALLS = 18
 FINAL = 2 * CALLS
 TABLE = (
-    (1, 2, 5, 8, 11, 14, 17, 20, 23, 26, 29, 32),
-    (3, 4, 7, 10, 13, 16, 19, 22, 25, 28, 31, 34),
-    (5, 6, 9, 12, 15, 18, 21, 24, 27, 30, 33, 36),
-    (7, 8, 11, 14, 17, 20, 23, 26, 29, 32, 35, 37),
-    (15, 16, 19, 22, 25, 28, 31, 34, 36, 37, 38, 39),
-    (17, 18, 21, 24, 27, 30, 33, 36, 37, 38, 39, 40),
-    (19, 20, 23, 26, 29, 32, 35, 37, 38, 39, 40, 41),
-    (21, 22, 25, 28, 31, 34, 36, 38, 39, 40, 41, 42),
-    (23, 24, 27, 30, 33, 36, 37, 39, 40, 41, 42, 43),
-    (25, 26, 29, 32, 35, 37, 38, 40, 41, 42, 43, 44),
+    (1, 2, 5, 8, 11, 14, 16, 18, 21, 24, 27, 30),
+    (3, 4, 7, 10, 13, 16, 18, 20, 23, 26, 29, 32),
+    (5, 6, 9, 12, 15, 18, 20, 22, 25, 28, 31, 34),
+    (7, 8, 11, 14, 17, 20, 22, 24, 27, 30, 33, 36),
+    (15, 16, 19, 22, 25, 28, 30, 32, 35, 36, 37, 38),
+    (17, 18, 21, 24, 27, 30, 32, 34, 36, 37, 38, 39),
+    (19, 20, 23, 26, 29, 32, 34, 36, 37, 38, 39, 40),
+    (21, 22, 25, 28, 31, 34, 36, 37, 38, 39, 40, 41),
+    (23, 24, 27, 30, 33, 36, 37, 38, 39, 40, 41, 42),
+    (25, 26, 29, 32, 35, 37, 38, 39, 40, 41, 42, 43),
     (33, 34, 36, 37, 38, 39, 40, 41, 42, 43, 44, 45),
     (35, 36, 37, 38, 39, 40, 41, 42, 43, 44, 45, 46),
 )
@@ -219,7 +219,7 @@
             ATT[layer, :, lanes] = jnp.concatenate(outs, axis=0).T.astype(BF16)
             return 0
 
-        lax.fori_loop(0, PAIRS, pair, 0)
+        lax.fori_loop(0, PAIRS, pair, 0, unroll=3)
         keep(2, layer, LSE, lses)
         keep(3, layer, ATT, atts)
         ready(OUT)
@@ -241,7 +241,7 @@
             ACC[rows, :] = y + SM[layer, B_DOWN]
             return 0
 
-        lax.fori_loop(0, tokens // 256, first_norm, 0)
+        lax.fori_loop(0, tokens // 256, first_norm, 0, unroll=2)
         keep(4, layer, N1, n1s)
         keep(5, layer, NB, nbs)
 
@@ -259,7 +259,7 @@
                 ACC[:, cols] += dot(ACT[...], W[layer, 2 * f, :, cols])
             return 0
 
-        lax.fori_loop(0, CHUNKS, ffn, 0)
+        lax.fori_loop(0, CHUNKS, ffn, 0, unroll=2)
         keep(6, layer, U, us)
 
         def second_norm(c, _):
@@ -270,7 +270,7 @@
             X[layer + 1, rows, :] = (n * SM[layer, G_FFN] + SM[layer, B_FFN]).astype(BF16)
             return 0
 
-        lax.fori_loop(0, tokens // 256, second_norm, 0)
+        lax.fori_loop(0, tokens // 256, second_norm, 0, unroll=2)
         keep(7, layer, N2, n2s)
         keep(8, layer, RS, rss)
 
@@ -325,9 +325,7 @@
 
     def view(self, job, start, size):
         block, typ = job
-        rows = pl.ds(pl.multiple_of(start, 16), size)
-        cols = pl.ds(pl.multiple_of(typ * THIRD, 128), THIRD)
-        return self.G.at[block, rows, cols]
+        return self.G.at[block, typ, pl.ds(pl.multiple_of(start, 16), size), :]
 
     def landing(self, job, start, size):
         block, typ = job
@@ -528,7 +526,8 @@
     def fetch(self, o):
         return pltpu.make_async_copy(self.peer_buf.at[o], self.ST, self.load.at[0])
 
-    def result(self, o, dst, remote):
+    def result(self, o, remote):
+        dst = self.outs.at[o % OWN * 2 + self.sec]
         if remote:
             return pltpu.make_async_remote_copy(
                 self.G.at[o],
@@ -541,32 +540,21 @@
         return pltpu.make_async_copy(self.G.at[o], dst, self.out.at[o])
 
     def output(self, o):
-        grad_q, grad_o, grad_i, grad_d = self.outs
-        layer, b = 1 - o // OWN, o % OWN * 2 + self.sec
-
-        def to(dst):
-            pl.when(layer == self.sec)(lambda: self.result(o, dst, False).start())
-            pl.when(layer != self.sec)(lambda: self.result(o, dst, True).start())
-
-        chunk = pl.ds(pl.multiple_of(b // 2 % CHUNKS * D, D), D)
-        third = pl.ds(pl.multiple_of(jnp.maximum(b - QKV, 0) * D, D), D)
-        pl.when((b < OUT) & (b % 2 == 0))(lambda: to(grad_d.at[chunk, :]))
-        pl.when((b < OUT) & (b % 2 == 1))(lambda: to(grad_i.at[:, chunk]))
-        pl.when(b == OUT)(lambda: to(grad_o))
-        pl.when(b > OUT)(lambda: to(grad_q.at[:, third]))
+        layer = 1 - o // OWN
+        pl.when(layer == self.sec)(lambda: self.result(o, False).start())
+        pl.when(layer != self.sec)(lambda: self.result(o, True).start())
 
     def wait_output(self, o):
-        grad_o = self.outs[1]
         layer = 1 - o // OWN
 
         @pl.when(layer == self.sec)
         def _():
-            self.result(o, grad_o, False).wait()
-            self.result(o, grad_o, True).wait_recv()
+            self.result(o, False).wait()
+            self.result(o, True).wait_recv()
 
         @pl.when(layer != self.sec)
         def _():
-            self.result(o, grad_o, True).wait_send()
+            self.result(o, True).wait_send()
 
     def step(self, o, k):
         if k == 0:
@@ -575,14 +563,14 @@
             return
         if k == 1:
             self.fetch(o).wait()
-            g, stage = self.G.at[o], self.ST
 
             def body(i, _):
-                rows = pl.ds(pl.multiple_of(i * 48, 48), 48)
-                g[rows, :] = g[rows, :] + stage[rows, :]
+                rows = pl.ds(pl.multiple_of(i % 8 * 96, 96), 96)
+                third = i // 8
+                self.G[o, third, rows, :] = self.G[o, third, rows, :] + self.ST[third, rows, :]
                 return 0
 
-            lax.fori_loop(0, D // 48, body, 0)
+            lax.fori_loop(0, 24, body, 0)
 
         def advance(kind, typ):
             ops = self.plan((o, typ), kind, typ)
@@ -603,12 +591,21 @@
 
     def slot(self, t):
         for k in reversed(range(self.steps)):
-            o, valid = jnp.int32(0), False
-            for block, times in enumerate(self.table):
-                due = t == times[k]
-                o = jnp.where(due, block, o)
-                valid = valid | due
-            pl.when(valid)(functools.partial(self.step, o, k))
+            times = [row[k] for row in self.table]
+            words = []
+            for w in range(times[-1] // 31 + 1):
+                words.append(sum(1 << (time - 31 * w) for time in times if 0 <= time - 31 * w < 31))
+            word = jnp.int32(words[-1])
+            for w in reversed(range(len(words) - 1)):
+                word = jnp.where(t < 31 * (w + 1), jnp.int32(words[w]), word)
+
+            @pl.when(((word >> (t % 31)) & 1 == 1) & (t <= times[-1]))
+            def _(k=k, times=times):
+                o = jnp.int32(0)
+                for time in times[:-1]:
+                    o = o + jnp.where(t > time, 1, 0)
+                self.step(o, k)
+
 
     @property
     def slots(self):
@@ -618,7 +615,7 @@
 def backward_kernel(
     dp_size, rep_size,
     cot, segs, wall, xs, qkvs, lses, atts, n1s, nbs, us, n2s, rss, tabs, biases, smalls,
-    grad_q, grad_o, grad_i, grad_d, grad_small, ing, peer_buf,
+    blocks, grad_small, ing, peer_buf,
     G, RB, ST, WR, UP, N2, NB, DB, DJ, N1, ATT, QK, U, DAT, DN, TAB, BIAS, RS, LSE, SM, SG, SB, SP,
     wsem, lsem, usem, send, recv, load, out, out_recv, peer_send, peer_recv, gsem, ssend, srecv, sync,
 ):
@@ -628,7 +625,7 @@
     peer = {"section": 1 - sec}
     tokens = UP.shape[0]
     sums = Blocks(
-        G, RB, ST, peer_buf, (grad_q, grad_o, grad_i, grad_d),
+        G, RB, ST, peer_buf, blocks,
         (send, recv, load, out, out_recv, peer_recv, peer_send, sync), dp, rep, dp_size, rep_size,
     )
 
@@ -714,7 +711,7 @@
             t = jnp.where(mine, o, BLOCKS + o % 2)
             for c in range(3):
                 cols = slice(c * 256, (c + 1) * 256)
-                G[t, :, cols] = dot_tn(lhs[...], rhs[:, cols]).astype(BF16)
+                G[t, c] = dot_tn(lhs[...], rhs[:, cols]).astype(BF16)
 
             pl.when(~mine)(lambda: sums.peer_block(o).start())
 
@@ -921,20 +918,26 @@
 
 
 RING = 6
-ROWS = 256
 
 
 def convert_kernel(
-    grad_q, grad_o, grad_i, grad_d, small,
+    blocks, small,
     out_q, out_o, out_i, out_d, b_q, b_o, g_a, b_a, b_i, b_d, g_f, b_f,
     LOW, HIGH, isem, osem,
 ):
     tiles = []
-    for src, dst in ((grad_q, out_q), (grad_o, out_o), (grad_i, out_i), (grad_d, out_d)):
-        for r in range(src.shape[0] // ROWS):
-            for c in range(src.shape[1] // D):
-                part = (pl.ds(r * ROWS, ROWS), pl.ds(c * D, D))
-                tiles.append((src.at[part], dst.at[0, part[0], part[1]]))
+    for b in range(BLOCKS):
+        for c in range(3):
+            cols = pl.ds(c * THIRD, THIRD)
+            if b < OUT and b % 2 == 0:
+                dst = out_d.at[0, pl.ds(b // 2 * D, D), cols]
+            elif b < OUT:
+                dst = out_i.at[0, :, pl.ds(b // 2 * D + c * THIRD, THIRD)]
+            elif b == OUT:
+                dst = out_o.at[0, :, cols]
+            else:
+                dst = out_q.at[0, :, pl.ds((b - QKV) * D + c * THIRD, THIRD)]
+            tiles.append((blocks.at[b, c], dst))
     reads = [pltpu.make_async_copy(src, LOW.at[i % RING], isem.at[i % RING]) for i, (src, _) in enumerate(tiles)]
     writes = [pltpu.make_async_copy(HIGH.at[i % RING], dst, osem.at[i % RING]) for i, (_, dst) in enumerate(tiles)]
     for i in range(RING):
@@ -948,11 +951,11 @@
             writes[i - RING].wait()
 
         def body(r, _, at=i % RING):
-            rows = pl.ds(pl.multiple_of(r * 64, 64), 64)
+            rows = pl.ds(pl.multiple_of(r * 192, 64), 192)
             HIGH[at, rows, :] = LOW[at, rows, :].astype(F32)
             return 0
 
-        lax.fori_loop(0, ROWS // 64, body, 0)
+        lax.fori_loop(0, 4, body, 0)
         writes[i].start()
         if i + RING < len(tiles):
             reads[i + RING].start()
@@ -1031,20 +1034,17 @@
     out = pl.pallas_call(
         functools.partial(backward_kernel, dp_size, rep_size),
         out_shape=(
-            shape(D, 3 * D),
-            shape(D, D),
-            shape(D, CHUNKS * D),
-            shape(CHUNKS * D, D),
+            shape(BLOCKS, 3, D, THIRD),
             shape(SMALL, 1, D, dtype=F32),
             shape(2, tokens, D),
-            shape(BLOCKS, D, D),
+            shape(BLOCKS, 3, D, THIRD),
         ),
         in_specs=[anywhere, in_vmem] + [anywhere] * 13,
-        out_specs=(anywhere,) * 7,
+        out_specs=(anywhere,) * 4,
         scratch_shapes=[
-            mem(BLOCKS + 2, D, D),
+            mem(BLOCKS + 2, 3, D, THIRD),
             mem(ring, 3, landing, THIRD),
-            mem(D, D),
+            mem(3, D, THIRD),
             mem(4, D, D),
             mem(tokens, D),
             mem(tokens, D),
@@ -1083,25 +1083,25 @@
         compiler_params=pltpu.CompilerParams(collective_id=1, has_side_effects=True, vmem_limit_bytes=VMEM_LIMIT),
         name="backward",
     )(cotangent, segments, wall, xs, qkvs, lses, atts, n1s, nbs, us, n2s, rss, tabs, biases, smalls)
-    grad_q, grad_o, grad_i, grad_d, grad_small, ing, _ = out
+    blocks, grad_small, ing, _ = out
     vectors = (3 * D, D, D, D, CHUNKS * D, D, D, D)
     grads = pl.pallas_call(
         convert_kernel,
         out_shape=(
-            *(shape(1, *grad.shape, dtype=F32) for grad in (grad_q, grad_o, grad_i, grad_d)),
+            *(shape(1, *dims, dtype=F32) for dims in ((D, 3 * D), (D, D), (D, CHUNKS * D), (CHUNKS * D, D))),
             *(shape(1, size, dtype=F32) for size in vectors),
         ),
-        in_specs=[anywhere] * 4 + [in_vmem],
+        in_specs=[anywhere, in_vmem],
         out_specs=(anywhere,) * 4 + (in_vmem,) * 8,
         scratch_shapes=[
-            mem(RING, ROWS, D),
-            mem(RING, ROWS, D, dtype=F32),
+            mem(RING, D, THIRD),
+            mem(RING, D, THIRD, dtype=F32),
             dma((RING,)),
             dma((RING,)),
         ],
         compiler_params=pltpu.CompilerParams(vmem_limit_bytes=VMEM_LIMIT),
         name="convert",
-    )(grad_q, grad_o, grad_i, grad_d, grad_small)
+    )(blocks, grad_small)
     grad_q, grad_o, grad_i, grad_d, b_q, b_o, g_a, b_a, b_i, b_d, g_f, b_f = grads
     return acts[None], ing[None], grad_q, b_q, grad_o, b_o, g_a, b_a, grad_i, b_i, grad_d, b_d, g_f, b_f
 

time: 305 us -> 300 us (0.984)
  Pallas kernels: 300 us -> 296 us
where the time goes in v3:
time: 300 us; the launch traced here: 299 us
  Pallas kernels  296 us (99%)
  local copies, waits for them, and re-layouts  3.1 us (1%)
    pallas_call x1, Pallas kernels, per_device(): pl.pallas_call(functools.partial(backward_kernel, dp_size, rep_size), out...  234 us
    pallas_call x1, Pallas kernels, per_device(): pl.pallas_call(forward_kernel, out_shape=(shape(2, BLOCKS, D, D), shape(2...  45.1 us
    pallas_call x1, Pallas kernels, per_device(): pl.pallas_call(convert_kernel, out_shape=(*(shape(1, *dims, dtype=F32) fo...  16.4 us

profile of v3, /device:TPU:0, one launch (start us, length us, event | category | flops | bytes accessed | tf_op | source)
XLA Modules:
  0.0 299.4 jit_solution(16256355618172677865)
XLA Ops:
  0.7 45.1 %forward.1 = (bf16[2,12,768,768]{3,2,1,0:T(8,128)(2,1)}, bf16[2,512,768]{2,1,0:T(8,128)(2,1)}, bf16[2,3,512,768]{3,2,1,0:T(8,128)(2,1)}, f32[2,6,8,512]{3,2,1,0:...) custom-call(bf16[2,512,768]{2,1,0:T(8,128)(2,1)} %inp.1, ...), custom_call_target="tpu_custom_call" | custom-call | tf_op jit(solution)/shard_map/forward/pallas_call | solution.py:981
  45.8 234.1 %backward.1 = (bf16[12,3,768,256]{3,2,1,0:T(8,128)(2,1)}, f32[16,1,768]{2,1,0:T(1,128)}, bf16[2,512,768]{2,1,0:T(8,128)(2,1)}, bf16[12,3,768,256]{3,2,1,0:T(8,128)(2,1)}) custom-call(bf16[2,512,768]{2,1,0:T(8,128)(2,1)} %cot.1, s32[2,512]{1,0:T(2,128)} %segs.3, bf16[2,12,768,768]{3,2,1,0:T(8,128)(2,1)} %get-tuple-element.44.wall, ...), custom_call_target="tpu_custom_call" | custom-call | tf_op jit(solution)/shard_map/backward/pallas_call | solution.py:1034
  279.9 0.0 copy-start
  279.9 16.4 %convert.1 = (f32[1,768,2304]{2,1,0:T(8,128)}, f32[1,768,768]{2,1,0:T(8,128)}, f32[1,768,3072]{2,1,0:T(8,128)}, f32[1,3072,768]{2,1,0:T(8,128)}, f32[1,2304]{1,0...) custom-call(bf16[12,3,768,256]{3,2,1,0:T(8,128)(2,1)} %get-tuple-ele, ...), custom_call_target="tpu_custom_call" | custom-call | tf_op jit(solution)/shard_map/convert/pallas_call | solution.py:1088
  296.3 0.0 copy-start.1
  296.3 0.0 copy-done
  296.3 1.1 copy.31
  297.5 0.8 copy-done.1
  298.3 1.1 copy.32
Async XLA Ops:
  279.9 16.5 %copy-start = (bf16[2,512,768]{2,1,0:T(8,128)(2,1)S(1)}, bf16[2,512,768]{2,1,0:T(8,128)(2,1)}, u32[]{:S(2)}) copy-start(bf16[2,512,768]{2,1,0:T(8,128)(2,1)} %get-tuple-element.43) | copy-start | bytes 4718596
  296.3 2.0 copy-start.1

commit v4 on v3

--- a/solution.py
+++ b/solution.py
@@ -219,7 +219,7 @@
             ATT[layer, :, lanes] = jnp.concatenate(outs, axis=0).T.astype(BF16)
             return 0
 
-        lax.fori_loop(0, PAIRS, pair, 0, unroll=3)
+        lax.fori_loop(0, PAIRS, pair, 0, unroll=6)
         keep(2, layer, LSE, lses)
         keep(3, layer, ATT, atts)
         ready(OUT)
@@ -339,7 +339,7 @@
         )
 
     def combine(self, job, start, place, size, add):
-        step = 96 if size % 96 == 0 else 48
+        step = next(n for n in (192, 96, 48) if size % n == 0)
         g = self.view(job, start, size)
         r = self.landing(job, place, size)
 
@@ -565,12 +565,12 @@
             self.fetch(o).wait()
 
             def body(i, _):
-                rows = pl.ds(pl.multiple_of(i % 8 * 96, 96), 96)
-                third = i // 8
+                rows = pl.ds(pl.multiple_of(i % 4 * 192, 96), 192)
+                third = i // 4
                 self.G[o, third, rows, :] = self.G[o, third, rows, :] + self.ST[third, rows, :]
                 return 0
 
-            lax.fori_loop(0, 24, body, 0)
+            lax.fori_loop(0, 12, body, 0)
 
         def advance(kind, typ):
             ops = self.plan((o, typ), kind, typ)

time: 300 us -> 297 us (0.990)
  Pallas kernels: 296 us -> 293 us
where the time goes in v4:
time: 297 us
  Pallas kernels  293 us (99%)
  local copies, waits for them, and re-layouts  3.1 us (1%)
    pallas_call x1, Pallas kernels, per_device(): pl.pallas_call(functools.partial(backward_kernel, dp_size, rep_size), out...  233 us
    pallas_call x1, Pallas kernels, per_device(): pl.pallas_call(forward_kernel, out_shape=(shape(2, BLOCKS, D, D), shape(2...  43.3 us
    pallas_call x1, Pallas kernels, per_device(): pl.pallas_call(convert_kernel, out_shape=(*(shape(1, *dims, dtype=F32) fo...  16.4 us

profile of v4, /device:TPU:0, one launch (start us, length us, event | category | flops | bytes accessed | tf_op | source)
XLA Modules:
  0.0 296.8 jit_solution(15670253289028782574)
XLA Ops:
  0.7 43.3 %forward.1 = (bf16[2,12,768,768]{3,2,1,0:T(8,128)(2,1)}, bf16[2,512,768]{2,1,0:T(8,128)(2,1)}, bf16[2,3,512,768]{3,2,1,0:T(8,128)(2,1)}, f32[2,6,8,512]{3,2,1,0:...) custom-call(bf16[2,512,768]{2,1,0:T(8,128)(2,1)} %inp.1, ...), custom_call_target="tpu_custom_call" | custom-call | tf_op jit(solution)/shard_map/forward/pallas_call | solution.py:981
  44.0 233.3 %backward.1 = (bf16[12,3,768,256]{3,2,1,0:T(8,128)(2,1)}, f32[16,1,768]{2,1,0:T(1,128)}, bf16[2,512,768]{2,1,0:T(8,128)(2,1)}, bf16[12,3,768,256]{3,2,1,0:T(8,128)(2,1)}) custom-call(bf16[2,512,768]{2,1,0:T(8,128)(2,1)} %cot.1, s32[2,512]{1,0:T(2,128)} %segs.3, bf16[2,12,768,768]{3,2,1,0:T(8,128)(2,1)} %get-tuple-element.44.wall, ...), custom_call_target="tpu_custom_call" | custom-call | tf_op jit(solution)/shard_map/backward/pallas_call | solution.py:1034
  277.3 0.0 copy-start
  277.3 16.4 %convert.1 = (f32[1,768,2304]{2,1,0:T(8,128)}, f32[1,768,768]{2,1,0:T(8,128)}, f32[1,768,3072]{2,1,0:T(8,128)}, f32[1,3072,768]{2,1,0:T(8,128)}, f32[1,2304]{1,0...) custom-call(bf16[12,3,768,256]{3,2,1,0:T(8,128)(2,1)} %get-tuple-ele, ...), custom_call_target="tpu_custom_call" | custom-call | tf_op jit(solution)/shard_map/convert/pallas_call | solution.py:1088
  293.7 0.0 copy-start.1
  293.7 0.0 copy-done
  293.7 1.1 copy.31
  294.9 0.8 copy-done.1
  295.7 1.1 copy.32
Async XLA Ops:
  277.3 16.5 %copy-start = (bf16[2,512,768]{2,1,0:T(8,128)(2,1)S(1)}, bf16[2,512,768]{2,1,0:T(8,128)(2,1)}, u32[]{:S(2)}) copy-start(bf16[2,512,768]{2,1,0:T(8,128)(2,1)} %get-tuple-element.43) | copy-start | bytes 4718596
  293.7 2.0 copy-start.1
